TPU v7x, 32 devices: a whole 2x2x4 slice. The times are simulated.
32 devices in a mesh: groups: 2 (over y), row: 8 (over z, x), col: 2 (over core).
Axes of the slice: x: 2, y: 2, z: 4, core: 2. Of those that a mesh axis runs over, the one named last changes fastest.
Arguments:
- cot: float32 [24576, 12288], P(('groups', 'row'), 'col'), parts along dimension 0
- panel_late: bfloat16 [24576, 512], P(('groups', 'row', 'col')), parts along dimension 0, may hold values from -0.0546875 to 0.0546875
- panel_early: bfloat16 [24576, 512], P(('groups', 'row', 'col')), parts along dimension 0, may hold values from -0.0546875 to 0.0546875
- inv_late: float32 [1024, 512], P('groups'), parts along dimension 0, as said below
- inv_early: float32 [1024, 512], P('groups'), parts along dimension 0, as said below
Outputs:
- late_cot: float32 [24576, 512], P(('groups', 'row', 'col')), parts along dimension 0
- early_cot: float32 [24576, 512], P(('groups', 'row', 'col')), parts along dimension 0
- late_diag: float32 [1024, 512], P(('groups', 'row')), parts along dimension 0
- early_diag: float32 [1024, 512], P(('groups', 'row')), parts along dimension 0
There are 2 independent parts, one for each index of `groups`. A program takes and returns all parts, laid end to end along the dimension named above; each array names one. Nothing has to cross between parts.
Inputs may be any that keep to these rules, and one draw needn't show every extreme that they name: inv_late is upper triangular with a diagonal of 1 to 2. inv_early is upper triangular with a diagonal of 1 to 2.
All inputs are finite; a program needn't handle non-finite values.
Results may differ from a plain program's by a relative error of at most 0.0003.
Values may be sent and summed in bfloat16 or wider, within the bound.
No kernel may reach another device: no remote copies, remote signals or barrier semaphores. Data moves between devices by JAX's collectives and lax.ppermute only.
A program may use at most 128 MiB of HBM per device.

v0:
```python
from functools import partial

import jax
import jax.numpy as jnp
from jax import lax
from jax.sharding import PartitionSpec as P


def from_root(value, axis, source):
    kept = jnp.where(lax.axis_index(axis) == source, value, 0).astype(value.dtype)
    return lax.psum(kept, axis)


def highest(left, right):
    return jnp.dot(left, right, precision=lax.Precision.HIGHEST, preferred_element_type=jnp.float32)


def inner_rows(left, right):
    return lax.dot_general(
        left,
        right,
        (((0,), (0,)), ((), ())),
        precision=lax.Precision.HIGHEST,
        preferred_element_type=jnp.float32,
    )


def accumulate_cols(matrix, running, piece_rows, start):
    return highest(matrix, piece_rows.astype(jnp.float32))


def per_device(cot, panel_late, panel_early, inv_late, inv_early):
    strip_rows = cot.shape[0]
    piece_rows = panel_late.shape[0]
    panel_width = panel_late.shape[1]
    n_rows = lax.axis_size("row")
    row_id = lax.axis_index("row")
    col_id = lax.axis_index("col")
    own_start = row_id * strip_rows + col_id * piece_rows
    positions = own_start + jnp.arange(piece_rows, dtype=jnp.int32)
    trailing = (positions >= panel_width)[:, None]
    late_masked = jnp.where(trailing, panel_late, jnp.zeros_like(panel_late))
    fold_cols = partial(accumulate_cols, cot)
    diag_rows = panel_width // n_rows
    late_part = fold_cols(
        jnp.zeros((strip_rows, panel_width), jnp.float32),
        lax.all_gather(late_masked, "row", axis=0, tiled=True),
        jnp.int32(0),
    )
    late_grad = lax.psum_scatter(late_part, "col", scatter_dimension=0, tiled=True)
    early_base = None
    late_grad = jnp.where(trailing, late_grad, jnp.float32(0.0))
    late_cot = -2.0 * highest(late_grad, inv_late.T)
    late_f = late_masked.astype(jnp.float32)
    early_f = panel_early.astype(jnp.float32)
    late_term = -inner_rows(late_cot, late_f)
    cross_term = inner_rows(late_cot, early_f)
    early_strip = lax.all_gather(panel_early, "col", axis=0, tiled=True)
    root_count = -(-panel_width // strip_rows)

    def collect(index, buffer):
        received = from_root(early_strip, "row", index)
        return lax.dynamic_update_index_in_dim(buffer, received, index, 0)

    top_buffer = lax.fori_loop(
        0, root_count, collect, jnp.zeros((root_count, strip_rows, panel_width), jnp.bfloat16)
    )
    top_block = top_buffer.reshape(root_count * strip_rows, panel_width)[:panel_width].astype(
        jnp.float32
    )
    late_full, cross_full = lax.psum((late_term, cross_term), ("row", "col"))
    symmetric = 0.5 * (late_full + late_full.T)
    corner = cross_full + highest(symmetric, top_block)
    late_diag = lax.dynamic_slice_in_dim(late_full, row_id * diag_rows, diag_rows, 0)
    corner_padded = jnp.concatenate(
        [corner, jnp.zeros((piece_rows, panel_width), jnp.float32)], axis=0
    )
    corner_rows = lax.dynamic_slice_in_dim(
        corner_padded, jnp.minimum(own_start, panel_width), piece_rows, 0
    )
    early_part = fold_cols(
        jnp.zeros((strip_rows, panel_width), jnp.float32),
        lax.all_gather(panel_early, "row", axis=0, tiled=True),
        jnp.int32(0),
    )
    early_base = lax.psum_scatter(early_part, "col", scatter_dimension=0, tiled=True)
    early_grad = early_base + highest(late_cot, top_block) + corner_rows
    early_cot = -2.0 * highest(early_grad, inv_early.T)
    early_term = -inner_rows(early_cot, early_f)
    early_whole = lax.psum(early_term, ("row", "col"))
    early_diag = lax.dynamic_slice_in_dim(early_whole, row_id * diag_rows, diag_rows, 0)
    return (late_cot, early_cot, late_diag, early_diag)


def solution(mesh):
    return jax.shard_map(
        per_device,
        mesh=mesh,
        in_specs=(
            P(("groups", "row"), "col"),
            P(("groups", "row", "col"), None),
            P(("groups", "row", "col"), None),
            P("groups", None),
            P("groups", None),
        ),
        out_specs=(
            P(("groups", "row", "col"), None),
            P(("groups", "row", "col"), None),
            P(("groups", "row"), None),
            P(("groups", "row"), None),
        ),
        check_vma=False,
    )
```

profile of v0, /device:TPU:0, one launch (start us, length us, event | category | flops | bytes accessed | tf_op | source)
XLA Modules:
  0.0 576.0 jit_solution(12210242290867226964)
XLA Ops:
  7.2 2.3 broadcast_select_fusion.1
  9.6 0.7 all-gather.8.cloned.1.call-update
  10.4 101.6 %all-gather.4.cloned.1.call-done = bf16[6144,512]{1,0:T(8,128)(2,1)} async-done(((bf16[768,512]{1,0:T(8,128)(2,1)}), bf16[6144,512]{1,0:T(8,128)(2,1)}) %all-gather.4.cloned.1.call-update) | async-done | bytes 6291472 | tf_op jit(solution)/shard_map/all_gather | solution.py:47
  112.0 35.9 %convolution_bitcast_fusion = f32[1536,512]{1,0:T(8,128)} fusion(bf16[6144,512]{1,0:T(8,128)(2,1)} %all-gather.4.cloned.1.call-done, f32[1536,6144]{1,0:T(8,128)} %param.5), kind=kOutput, calls=%fused_computation | convolution fusion | flops 57982058496 | bytes 47185920 | tf_op jit(solution)/shard_map/dot_general | solution.py:15
  148.0 0.5 all-gather.6.cloned.1.call-update
  148.6 2.7 broadcast_select_fusion
  151.5 5.7 reduce-scatter.3.cloned.1.call-done
  157.1 4.1 fusion.6
  161.3 4.1 convolution_negate_fusion.1
  165.4 2.4 fusion.25
  168.1 91.5 %all-gather.6.cloned.1.call-done = bf16[6144,512]{1,0:T(8,128)(2,1)} async-done(((bf16[768,512]{1,0:T(8,128)(2,1)}), bf16[6144,512]{1,0:T(8,128)(2,1)}) %all-gather.6.cloned.1.call-update) | async-done | bytes 6291472 | tf_op jit(solution)/shard_map/all_gather | solution.py:83
  259.6 35.9 %fusion.24 = f32[1536,512]{1,0:T(8,128)} fusion(f32[1536,6144]{1,0:T(8,128)} %param.5, bf16[6144,512]{1,0:T(8,128)(2,1)} %all-gather.6.cloned.1.call-done), kind=kOutput, calls=%fused_computation.29 | convolution fusion | flops 57982058496 | bytes 47185920 | tf_op jit(solution)/shard_map/dot_general | solution.py:15
  295.9 55.2 %all-reduce.6.cloned.1.call-done = bf16[1536,512]{1,0:T(8,128)(2,1)} async-done(((bf16[1536,512]{1,0:T(8,128)(2,1)}), bf16[1536,512]{1,0:T(8,128)(2,1)}) %all-reduce.6.cloned.1.call-update) | async-done | bytes 1572880 | tf_op jit(solution)/shard_map/while/body/eval_jaxpr/psum | solution.py:11
  351.1 3.6 fusion.18
  354.7 97.7 %all-reduce.10.cloned.1.call-done = (f32[512,512]{1,0:T(8,128)}, f32[512,512]{1,0:T(8,128)}) async-done(((f32[512,512]{1,0:T(8,128)}, f32[512,512]{1,0:T(8,128)}), (f32[512,512]{1,0:T(8,128)}, f32[512,512]{1,0:T(8,128)})) %all-reduce.10.cloned.1.call-update) | async-done | bytes 2097168 | tf_op jit(solution)/shard_map/psum | solution.py:71
  452.4 2.6 copy.9
  455.0 3.8 convolution_add_fusion
  458.8 6.2 %reduce-scatter.5.cloned.1.call-done = f32[768,512]{1,0:T(8,128)} async-done(((f32[1536,512]{1,0:T(8,128)}), f32[768,512]{1,0:T(8,128)}) %reduce-scatter.5.cloned.1.call-update) | async-done | bytes 1572880 | tf_op jit(solution)/shard_map/reduce_scatter | solution.py:86
  465.0 4.8 fusion.9
  469.8 1.1 copy-done.5
  471.0 2.5 convolution_negate_fusion
  473.5 1.6 constant_dynamic-slice_fusion.1
  475.0 92.5 %all-reduce.8.cloned.1.call-done = f32[512,512]{1,0:T(8,128)} async-done(((f32[512,512]{1,0:T(8,128)}), f32[512,512]{1,0:T(8,128)}) %all-reduce.8.cloned.1.call-update) | async-done | bytes 1048592 | tf_op jit(solution)/shard_map/psum | solution.py:90
  567.5 1.6 constant_dynamic-slice_fusion
  (29 shorter events, 1.1 us)
Async XLA Ops:
  7.2 150.0 %copy-start = (f32[512,512]{1,0:T(8,128)S(1)}, f32[512,512]{1,0:T(8,128)}, u32[]{:S(2)}) copy-start(f32[512,512]{1,0:T(8,128)} %param.8) | copy-start | bytes 3145732
  7.2 104.8 %all-gather.4.cloned.1.call-start = ((), (), s32[]{:S(2)}) async-start(), calls=%async_computation.2 | async-start | bytes 7077888 | tf_op jit(solution)/shard_map/all_gather | solution.py:47
  9.6 139.0 %all-gather.8.cloned.1.call-start = ((), (), s32[]{:S(2)}) async-start(), calls=%async_computation.6 | async-start | bytes 2359296 | tf_op jit(solution)/shard_map/all_gather | solution.py:58
  10.3 146.8 %reduce-scatter.3.cloned.1.call-start = ((), (), s32[]{:S(2)}) async-start(), calls=%async_computation.3 | async-start | bytes 4718592 | tf_op jit(solution)/shard_map/reduce_scatter | solution.py:50
  147.9 111.7 %all-gather.6.cloned.1.call-start = ((), (), s32[]{:S(2)}) async-start(), calls=%async_computation.4 | async-start | bytes 7077888 | tf_op jit(solution)/shard_map/all_gather | solution.py:83
  148.5 202.7 %all-reduce.6.cloned.1.call-start = ((), (), s32[]{:S(2)}) async-start(), calls=%async_computation.7 | async-start | bytes 3145728 | tf_op jit(solution)/shard_map/while/body/eval_jaxpr/psum | solution.py:11
  151.3 301.1 %all-reduce.10.cloned.1.call-start = ((), (), s32[]{:S(2)}) async-start(), calls=%async_computation.9 | async-start | bytes 4194304 | tf_op jit(solution)/shard_map/psum | solution.py:71
  161.3 189.9 %copy-start.2 = (f32[768,512]{1,0:T(8,128)}, f32[768,512]{1,0:T(8,128)S(1)}, u32[]{:S(2)}) copy-start(f32[768,512]{1,0:T(8,128)S(1)} %fusion.6) | copy-start | bytes 4718596
  161.3 4.1 copy-start.3
  167.9 297.2 %reduce-scatter.5.cloned.1.call-start = ((), (), s32[]{:S(2)}) async-start(), calls=%async_computation.5 | async-start | bytes 4718592 | tf_op jit(solution)/shard_map/reduce_scatter | solution.py:86
  295.6 272.0 %all-reduce.8.cloned.1.call-start = ((), (), s32[]{:S(2)}) async-start(), calls=%async_computation.8 | async-start | bytes 2097152 | tf_op jit(solution)/shard_map/psum | solution.py:90
  452.4 2.6 copy-start.6
  455.0 10.0 %copy-start.4 = (f32[768,512]{1,0:T(8,128)S(1)}, f32[768,512]{1,0:T(8,128)}, u32[]{:S(2)}) copy-start(f32[768,512]{1,0:T(8,128)} %fusion.18) | copy-start | bytes 4718596
  469.8 1.1 copy-start.5
  471.0 98.2 %copy-start.1 = (f32[512,512]{1,0:T(8,128)S(1)}, f32[512,512]{1,0:T(8,128)}, u32[]{:S(2)}) copy-start(f32[512,512]{1,0:T(8,128)} %param.8) | copy-start | bytes 3145732
Sparse Core Ops, SparseCore 0:
  10.2 101.7 all-gather.3
  113.5 7.9 all-gather.7
  148.0 9.0 reduce-scatter.2
  159.4 100.1 all-gather.5
  264.0 87.0 all-reduce.5
  355.0 97.2 all-reduce.9
  454.6 10.3 reduce-scatter.4
  473.6 93.9 all-reduce.7
where the time goes:
time: 576 us
  waiting for transfers between devices  452 us (78%)
  matrix products  97.1 us (17%)
  between operations  14.2 us (2%)
  local copies, waits for them, and re-layouts  6.93 us (1%)
    all_gather x1, waiting for transfers between devices, per_device(): lax.all_gather(late_masked, 'row', axis=0, tiled=True)  102 us
    psum x1, waiting for transfers between devices, per_device(): late_full, cross_full = lax.psum((late_term, cross_term), ('row', 'col'))  97.7 us
    psum x1, waiting for transfers between devices, per_device(): early_whole = lax.psum(early_term, ('row', 'col'))  92.5 us
    all_gather x1, waiting for transfers between devices, per_device(): lax.all_gather(panel_early, 'row', axis=0, tiled=True)  91.5 us
    dot_general x6, matrix products, highest(): jnp.dot(left, right, precision=lax.Precision.HIGHEST, preferred_element_t...  88.1 us
    psum x1, waiting for transfers between devices, from_root(): return lax.psum(kept, axis)  55.2 us
  transfers between devices with their start and end apart: 8, of which 7 were waited for; matrix products, arithmetic and copies ran while one was open for 17% of the time, Pallas kernels for 0%

commit v1 on v0

v1 whole, which is shorter than its diff:
```python
import jax
import jax.numpy as jnp
from jax import lax
from jax.experimental import pallas as pl
from jax.experimental.pallas import tpu as pltpu
from jax.sharding import PartitionSpec as P

SWAP = [(0, 1), (1, 0)]


def high(left, right, contract=(1, 0)):
    return lax.dot_general(
        left,
        right,
        (((contract[0],), (contract[1],)), ((), ())),
        precision=lax.Precision.HIGH,
        preferred_element_type=jnp.float32,
    )


def highest(left, right):
    return jnp.dot(left, right, precision=lax.Precision.HIGHEST, preferred_element_type=jnp.float32)


def inner_rows(left, right):
    return lax.dot_general(
        left,
        right,
        (((0,), (0,)), ((), ())),
        precision=lax.Precision.HIGHEST,
        preferred_element_type=jnp.float32,
    )


def ring_order(n_rows):
    return list(range(0, n_rows, 2)) + list(range(n_rows - 1, 0, -2))


def flip(n, bit):
    return [(i, i ^ bit) for i in range(n)]


def sum_cols(value, col_id):
    half = value.shape[0] // 2
    low, high_rows = value[:half], value[half:]
    first = col_id == 0
    sent = jnp.where(first, high_rows, low)
    return jnp.where(first, low, high_rows) + lax.ppermute(sent, "col", SWAP)


def fold_cols(value, col_id, n_rows):
    block, width = value.shape[0] // n_rows, value.shape[1]
    value = value.reshape(n_rows, 2, block // 2, width)
    first = col_id == 0
    sent = jnp.where(first, value[:, 1], value[:, 0])
    return jnp.where(first, value[:, 0], value[:, 1]) + lax.ppermute(sent, "col", SWAP)


def scatter_step(value, row_id, n_rows, bit):
    pairs = value.reshape(-1, 2, *value.shape[1:])
    zero = (row_id & bit) == 0
    kept = jnp.where(zero, pairs[:, 0], pairs[:, 1])
    sent = jnp.where(zero, pairs[:, 1], pairs[:, 0])
    return kept + lax.ppermute(sent, "row", flip(n_rows, bit))


def scatter_rows(value, row_id, n_rows):
    bit = 1
    while bit < n_rows:
        value = scatter_step(value, row_id, n_rows, bit)
        bit *= 2
    return value[0]


def split(value):
    coarse = value.astype(jnp.bfloat16)
    return coarse, (value - coarse.astype(jnp.float32)).astype(jnp.bfloat16)


def product(left, right, contract):
    dims = (((contract[0],), (contract[1],)), ((), ()))

    def dot(a, b):
        return lax.dot_general(a, b, dims, preferred_element_type=jnp.float32)

    coarse, fine = split(left)
    if right.dtype == jnp.bfloat16:
        return dot(coarse, right) + dot(fine, right)
    right_coarse, right_fine = split(right)
    return dot(coarse, right_coarse) + (dot(coarse, right_fine) + dot(fine, right_coarse))


def piece_kernel(count, has_total, places, *refs):
    blocks, pieces = refs[:count], refs[count : 2 * count]
    total, out = refs[2 * count], refs[-1]
    acc = total[...] if has_total else None
    for block, piece in zip(blocks, pieces):
        for part in split(block[...]):
            term = jnp.dot(part, piece[...], preferred_element_type=jnp.float32)
            acc = term if acc is None else acc + term
    out[...] = acc


def add_pieces(total, matrix, pieces, places):
    rows, width = matrix.shape[0], pieces[0][0].shape[1]
    tile = 512 if rows % 512 == 0 else 256

    def columns(depth, index):
        return pl.BlockSpec((tile, depth), lambda i, where: (i, where[index]))

    def part(depth, block):
        return pl.BlockSpec((depth, width), lambda i, where: (block, 0))

    specs = [columns(depth, index) for _, _, depth, index in pieces]
    specs += [part(depth, block) for _, block, depth, _ in pieces]
    args = [matrix] * len(pieces) + [array for array, _, _, _ in pieces]
    line = pl.BlockSpec((tile, width), lambda i, where: (i, 0))
    aliases = {}
    if total is not None:
        aliases = {1 + len(args): 0}
        specs.append(line)
        args.append(total)
    depth = sum(p[2] for p in pieces)
    return pl.pallas_call(
        lambda *refs: piece_kernel(len(pieces), total is not None, *refs),
        out_shape=jax.ShapeDtypeStruct((rows, width), jnp.float32),
        grid_spec=pltpu.PrefetchScalarGridSpec(
            num_scalar_prefetch=1, grid=(rows // tile,), in_specs=specs, out_specs=line
        ),
        input_output_aliases=aliases,
        compiler_params=pltpu.CompilerParams(vmem_limit_bytes=40 * 1024 * 1024),
        cost_estimate=pl.CostEstimate(
            flops=8 * rows * depth * width, bytes_accessed=4 * rows * depth, transcendentals=0
        ),
    )(places, *args)


def late_kernel(grad, late, early, top, inv_late, inv_early, late_cot, both):
    width = late_cot.shape[1]
    cot = -2.0 * product(grad[...], inv_late[...], (1, 1))
    late_cot[...] = cot
    late_term = -product(cot, late[...], (0, 0))
    corner = product(cot, early[...], (0, 0))
    corner += product(0.5 * (late_term + late_term.T), top[...], (1, 0))
    both[:, :width] = late_term
    both[:, width:] = -2.0 * product(corner, inv_early[...], (1, 1))


def late_chain(grad, late, early, top, inv_late, inv_early):
    rows, width = grad.shape
    return pl.pallas_call(
        late_kernel,
        out_shape=(
            jax.ShapeDtypeStruct((rows, width), jnp.float32),
            jax.ShapeDtypeStruct((width, 2 * width), jnp.float32),
        ),
        compiler_params=pltpu.CompilerParams(vmem_limit_bytes=40 * 1024 * 1024),
        cost_estimate=pl.CostEstimate(
            flops=16 * rows * width * width, bytes_accessed=8 * rows * width, transcendentals=0
        ),
    )(grad, late, early, top, inv_late, inv_early)


def early_kernel(grad, early, share, inv_early, early_cot, early_term):
    cot = -2.0 * product(grad[...], inv_early[...], (1, 1))
    early_cot[...] = cot
    early_term[...] = share[...] - product(cot, early[...], (0, 0))


def early_chain(grad, early, share, inv_early):
    rows, width = grad.shape
    return pl.pallas_call(
        early_kernel,
        out_shape=(
            jax.ShapeDtypeStruct((rows, width), jnp.float32),
            jax.ShapeDtypeStruct((width, width), jnp.float32),
        ),
        compiler_params=pltpu.CompilerParams(vmem_limit_bytes=40 * 1024 * 1024),
        cost_estimate=pl.CostEstimate(
            flops=10 * rows * width * width, bytes_accessed=8 * rows * width, transcendentals=0
        ),
    )(grad, early, share, inv_early)


def ring_places(n_rows, row_id):
    order = ring_order(n_rows)
    where = [0] * n_rows
    for place, row in enumerate(order):
        where[row] = place
    entries = [(0, 1, 0)]
    for step in range(1, n_rows // 2):
        entries += [(-step, 1, 0), (step, 1, 0)]
    half_at = {}
    for step in range(1, n_rows // 2 + 1):
        for way, sign in ((0, -1), (1, 1)):
            for half in (0, 1):
                half_at[way, step, half] = len(entries)
                entries.append((sign * step, 2, half))
    offset, scale, shift = (jnp.array(part, jnp.int32) for part in zip(*entries))
    place = jnp.array(where, jnp.int32)[row_id]
    owner = jnp.array(order, jnp.int32)[(place + offset + n_rows) % n_rows]
    return owner, owner * scale + shift, half_at


def by_ring(cot, late_masked, panel_early, inv_late, inv_early, trailing, own_start):
    n_rows = lax.axis_size("row")
    row_id = lax.axis_index("row")
    col_id = lax.axis_index("col")
    piece_rows, width = late_masked.shape
    first = col_id == 0
    is_root = (row_id == 0) & first
    owner, places, half_at = ring_places(n_rows, row_id)
    half = piece_rows // 2
    mid = n_rows // 2
    local = jnp.arange(piece_rows, dtype=jnp.int32)[:, None]
    order = ring_order(n_rows)
    ahead = [(order[i], order[(i + 1) % n_rows]) for i in range(n_rows)]
    ways = (ahead, [(b, a) for a, b in ahead])
    tie = lax.optimization_barrier

    def lead(value, way):
        return value[:half] if way == 0 else value[half:]

    def rest(value, way):
        return value[half:] if way == 0 else value[:half]

    def send(held):
        return list(tie(tuple(lax.ppermute(h, "row", way) for h, way in zip(held, ways))))

    def kept(piece, index, start):
        zero = first & (owner[index] == 0) & (local[start : start + piece.shape[0]] < width)
        return jnp.where(zero, jnp.zeros_like(piece), piece)

    sent = jnp.where(is_root & (local < width), panel_early, late_masked)
    late_part = add_pieces(None, cot, [(late_masked, 0, piece_rows, 0)], places)
    early_part = add_pieces(None, cot, [(panel_early, 0, piece_rows, 0)], places)
    top = jnp.where(is_root, sent[:width], jnp.zeros_like(sent[:width]))
    held = [sent, sent]
    for step in range(1, mid):
        held = send(held)
        if step == 1:
            late_part, *held = tie((late_part, *held))
        else:
            late_part, early_part, *held = tie((late_part, early_part, *held))
        pieces = []
        for way, piece in enumerate(held):
            index = 2 * step - 1 + way
            top = jnp.where(first & (owner[index] == 0), piece[:width], top)
            pieces.append((kept(piece, index, 0), 0, piece_rows, index))
        late_part = add_pieces(late_part, cot, pieces, places)

    held = [jnp.concatenate([lead(h, w), lead(panel_early, w)]) for w, h in enumerate(held)]
    held = send(held)
    late_part, *held = tie((late_part, *held))
    far = [half_at[0, mid, 0], half_at[1, mid, 1]]
    whole = jnp.concatenate([h[:half] for h in held])
    top = jnp.where(first & (owner[far[0]] == 0), whole[:width], top)
    pieces = [(kept(h[:half], far[w], w * half), 0, half, far[w]) for w, h in enumerate(held)]
    late_part = add_pieces(late_part, cot, pieces, places)
    waiting = [(h, 1, half, half_at[w, 1, w]) for w, h in enumerate(held)]

    for step in range(1, mid):
        if step == 1:
            held = [jnp.concatenate([rest(panel_early, w), h[half:]]) for w, h in enumerate(held)]
        held = send(held)
        if step == 1:
            top = jnp.where(first, top, lax.ppermute(top, "col", [(0, 1)]))
            late_grad = jnp.where(trailing, sum_cols(late_part, col_id), jnp.float32(0.0))
            late_grad, top, *held = tie((late_grad, top, *held))
            late_cot, both = late_chain(late_grad, late_masked, panel_early, top, inv_late, inv_early)
            corner_cot = both[:, width:]
        elif step == 2:
            early_part, both, *held = tie((early_part, both, *held))
            both = fold_cols(both, col_id, n_rows)
        else:
            early_part, *held = tie((early_part, *held))
        for w, h in enumerate(held):
            waiting.append((h, 0, half, half_at[w, step, 1 - w]))
            waiting.append((h, 1, half, half_at[w, step + 1, w]))
        early_part = add_pieces(early_part, cot, waiting, places)
        waiting = []

    both = scatter_rows(both, row_id, n_rows)
    top_f = top.astype(jnp.float32)
    extra = high(late_cot, top_f)
    corner_share = -high(corner_cot, top_f, (0, 0))
    early_grad = sum_cols(early_part, col_id) + extra
    early_cot, early_term = early_chain(early_grad, panel_early, corner_share, inv_early)
    early_own = scatter_rows(fold_cols(early_term, col_id, n_rows), row_id, n_rows)
    own = both[:, width:]
    blocks = [own] + [lax.ppermute(own, "row", [(k, 0)]) for k in range(1, n_rows)]
    mine = jnp.stack([both[:, :width], early_own] + blocks)
    other = lax.ppermute(mine, "col", SWAP)
    joined = jnp.stack([jnp.where(first, mine, other), jnp.where(first, other, mine)], axis=1)
    joined = joined.reshape(n_rows + 2, -1, width)
    corner = jnp.where(is_root, joined[2:].reshape(width, width), jnp.float32(0.0))
    early_cot = jnp.concatenate([early_cot[:width] + corner, early_cot[width:]], axis=0)
    return (late_cot, early_cot, joined[0], joined[1])


def by_gather(cot, late_masked, panel_early, inv_late, inv_early, trailing, own_start):
    piece_rows, panel_width = late_masked.shape
    strip_rows = cot.shape[0]
    early_f = panel_early.astype(jnp.float32)
    col_id = lax.axis_index("col")
    late_all = lax.all_gather(late_masked, "row", axis=0, tiled=True)
    late_part = highest(cot, late_all.astype(jnp.float32))
    early_all = lax.all_gather(panel_early, "row", axis=0, tiled=True)
    early_part = highest(cot, early_all.astype(jnp.float32))
    strips = -(-panel_width // strip_rows)
    own_top = early_all[: strips * piece_rows].reshape(strips, piece_rows, panel_width)
    top_block = lax.all_gather(own_top, "col", axis=1).reshape(-1, panel_width)[:panel_width]
    top_block = top_block.astype(jnp.float32)
    late_grad = jnp.where(trailing, sum_cols(late_part, col_id), jnp.float32(0.0))
    late_cot = -2.0 * highest(late_grad, inv_late.T)
    late_term = -inner_rows(late_cot, late_masked.astype(jnp.float32))
    cross_term = inner_rows(late_cot, early_f)
    corner_term = cross_term + highest(0.5 * (late_term + late_term.T), top_block)
    corner = lax.psum(corner_term, ("row", "col"))
    corner_padded = jnp.concatenate(
        [corner, jnp.zeros((piece_rows, panel_width), jnp.float32)], axis=0
    )
    corner_rows = lax.dynamic_slice_in_dim(
        corner_padded, jnp.minimum(own_start, panel_width), piece_rows, 0
    )
    extra = highest(late_cot, top_block) + corner_rows
    early_grad = sum_cols(early_part, col_id) + extra
    early_cot = -2.0 * highest(early_grad, inv_early.T)
    early_term = -inner_rows(early_cot, early_f)
    late_diag, early_diag = (
        lax.psum(lax.psum_scatter(term, "row", scatter_dimension=0, tiled=True), "col")
        for term in (late_term, early_term)
    )
    return (late_cot, early_cot, late_diag, early_diag)


def per_device(cot, panel_late, panel_early, inv_late, inv_early):
    strip_rows = cot.shape[0]
    piece_rows, panel_width = panel_late.shape
    n_rows = lax.axis_size("row")
    own_start = lax.axis_index("row") * strip_rows + lax.axis_index("col") * piece_rows
    positions = own_start + jnp.arange(piece_rows, dtype=jnp.int32)
    trailing = (positions >= panel_width)[:, None]
    late_masked = jnp.where(trailing, panel_late, jnp.zeros_like(panel_late))
    few = n_rows <= 16 and n_rows & (n_rows - 1) == 0 and piece_rows >= panel_width
    plan = by_ring if few and piece_rows % 256 == 0 else by_gather
    return plan(cot, late_masked, panel_early, inv_late, inv_early, trailing, own_start)


def solution(mesh):
    return jax.shard_map(
        per_device,
        mesh=mesh,
        in_specs=(
            P(("groups", "row"), "col"),
            P(("groups", "row", "col"), None),
            P(("groups", "row", "col"), None),
            P("groups", None),
            P("groups", None),
        ),
        out_specs=(
            P(("groups", "row", "col"), None),
            P(("groups", "row", "col"), None),
            P(("groups", "row"), None),
            P(("groups", "row"), None),
        ),
        check_vma=False,
    )
```

time: 576 us -> 227 us (0.39)
  waiting for transfers between devices: 452 us -> 75.3 us
  matrix products: 97.1 us -> 4.87 us
  Pallas kernels: 0 us -> 80.9 us
  starting transfers between devices: 0.98 us -> 33.4 us
  other arithmetic: 4.95 us -> 20.4 us
  between operations: 14.2 us -> 6.6 us
    psum x3 -> x0, waiting for transfers between devices: 245 us -> none  [the longest x1 97.7 us: per_device(): late_full, cross_full = lax.psum((late_term, cross_term), ('row', 'col'))]
    all_gather x3 -> x0, waiting for transfers between devices: 193 us -> none  [the longest x1 102 us: per_device(): lax.all_gather(late_masked, 'row', axis=0, tiled=True)]
    dot_general x9 -> x2, matrix products: 97.1 us -> 4.87 us  [high(): lax.dot_general(left, right, (((contract[0],), (contract[1],)), ((), ()))...]
    pallas_call x0 -> x11, Pallas kernels: none -> 80.9 us  [the longest x9 74 us: add_pieces(): pl.pallas_call(lambda *refs: piece_kernel(len(pieces), total is not None,...]
    ppermute x0 -> x33, waiting for transfers between devices: none -> 75.3 us  [the longest x14 46.1 us: send(): lax.ppermute(h, 'row', way)]
    ppermute x0 -> x33, starting transfers between devices: none -> 33.4 us  [the longest x14 15.6 us: send(): lax.ppermute(h, 'row', way)]
    reduce_scatter x2 -> x0, waiting for transfers between devices: 11.9 us -> none  [the longest x1 6.22 us: per_device(): lax.psum_scatter(early_part, 'col', scatter_dimension=0, tiled=True)]
    select_n x2 -> x22, other arithmetic: 4.94 us -> 14 us  [the longest x6 3.31 us: kept(): return jnp.where(zero, jnp.zeros_like(piece), piece)]
  transfers between devices with their start and end apart: 8 -> 33, of which waited for: 7 -> 20; matrix products, arithmetic and copies ran while one was open for 17% -> 9% of each run, Pallas kernels for 0% -> 33%
where the time goes in v1:
time: 227 us; the launch traced here: 226 us
  Pallas kernels  80.9 us (36%)
  waiting for transfers between devices  75.3 us (33%)
  starting transfers between devices  33.4 us (15%)
  other arithmetic  20.4 us (9%)
  between operations  6.6 us (3%)
  matrix products  4.87 us (2%)
  local copies, waits for them, and re-layouts  4.66 us (2%)
    pallas_call x9, Pallas kernels, add_pieces(): pl.pallas_call(lambda *refs: piece_kernel(len(pieces), total is not None,...  74 us
    ppermute x14, waiting for transfers between devices, send(): lax.ppermute(h, 'row', way)  46.1 us
    ppermute x6, waiting for transfers between devices, scatter_step(): return kept + lax.ppermute(sent, 'row', flip(n_rows, bit))  19.3 us
    ppermute x14, starting transfers between devices, send(): lax.ppermute(h, 'row', way)  15.6 us
    ppermute x7, starting transfers between devices, by_ring(): lax.ppermute(own, 'row', [(k, 0)])  9.03 us
    ppermute x7, waiting for transfers between devices, by_ring(): lax.ppermute(own, 'row', [(k, 0)])  7.83 us
    ppermute x6, starting transfers between devices, scatter_step(): return kept + lax.ppermute(sent, 'row', flip(n_rows, bit))  6.12 us
    dot_general x2, matrix products, high(): lax.dot_general(left, right, (((contract[0],), (contract[1],)), ((), ()))...  4.87 us
  transfers between devices with their start and end apart: 33, of which 20 were waited for; matrix products, arithmetic and copies ran while one was open for 9% of the time, Pallas kernels for 33%

profile of v1, /device:TPU:0, one launch (start us, length us, event | category | flops | bytes accessed | tf_op | source)
XLA Modules:
  0.0 226.1 jit_solution(4666027321167813345)
XLA Ops:
  0.7 2.8 %broadcast_select_fusion.3 = (bf16[768,512]{1,0:T(8,128)(2,1)}, bf16[768,512]{1,0:T(8,128)(2,1)}) fusion(bf16[768,512]{1,0:T(8,128)(2,1)} %early.3, pred[768]{0:T(1024)(128)(4,1)S(1)} %get-tuple-element.112, bf16[768,512]{1,0:T(8,128)(2,1)} %param.11, pred[768]{0:T(1024)(128)(4,1)S(1)} %get-tuple-element.113), kind=kLoop, calls=%fused_computation.26 | loop fusion | flops 786432 | bytes 3147264 | tf_op jit(solution)/shard_map/jit(_where)/select_n | solution.py:234
  3.5 3.0 %collective-permute-start = (bf16[768,512]{1,0:T(8,128)(2,1)}, bf16[768,512]{1,0:T(8,128)(2,1)}, u32[]{:S(2)}, u32[]{:S(2)}) collective-permute-start(bf16[768,512]{1,0:T(8,128)(2,1)} %get-tuple-element.90), channel_id=1, source_target_pairs={{0,4},{4,8},{8,12},{12,14},{14,10},{10,6},{6,2},{2,0},{1,5},{5,9},... | collective-permute-start | bytes 2359304 | tf_op jit(solution)/shard_map/ppermute | solution.py:228
  15.6 5.4 %shard_map.131.refs_13_ = f32[1536,512]{1,0:T(8,128)S(1)} custom-call(s32[23]{0:T(128)S(1)} %multiply_add_fusion.refs_0_, f32[1536,6144]{1,0:T(8,128)} %refs_4_.5, bf16[768,512]{1,0:T(8,128)(2,1)S(1)} %copy-done.2), custom_call_target="tpu_custom_call" | custom-call | flops 4831838208 | bytes 4718592 | tf_op jit(solution)/shard_map/pallas_call | solution.py:124
  22.1 5.4 %shard_map.129.refs_5_ = f32[1536,512]{1,0:T(8,128)S(1)} custom-call(s32[23]{0:T(128)S(1)} %multiply_add_fusion.refs_0_, f32[1536,6144]{1,0:T(8,128)} %refs_4_.5, bf16[768,512]{1,0:T(8,128)(2,1)S(1)} %copy-done.7), custom_call_target="tpu_custom_call" | custom-call | flops 4831838208 | bytes 4718592 | tf_op jit(solution)/shard_map/pallas_call | solution.py:124
  32.3 8.2 %shard_map.130.refs_5_ = f32[1536,512]{1,0:T(8,128)S(1)} custom-call(s32[23]{0:T(128)S(1)} %multiply_add_fusion.refs_0_, f32[1536,6144]{1,0:T(8,128)} %refs_4_.5, f32[1536,6144]{1,0:T(8,128)} %refs_4_.5, bf16[768,512]{1,0:T(8,128)(2,1)S(1)} %broadcast_select_fusion.4.refs_3_, ...), custom_call_target="tpu_custom_call", output_to_operand_aliasing={{}: (5, {})} | custom-call | flops 9663676416 | bytes 9437184 | tf_op jit(solution)/shard_map/pallas_call | solution.py:124
  40.4 6.4 %collective-permute-done.2 = bf16[768,512]{1,0:T(8,128)(2,1)S(1)} collective-permute-done((bf16[768,512]{1,0:T(8,128)(2,1)}, bf16[768,512]{1,0:T(8,128)(2,1)S(1)}, u32[]{:S(2)}, u32[]{:S(2)}) %collective-permute-start.2) | collective-permute-done | bytes 786464 | tf_op jit(solution)/shard_map/ppermute | solution.py:228
  50.6 8.2 %shard_map.132.refs_5_ = f32[1536,512]{1,0:T(8,128)S(1)} custom-call(s32[23]{0:T(128)S(1)} %multiply_add_fusion.refs_0_, f32[1536,6144]{1,0:T(8,128)} %refs_4_.5, f32[1536,6144]{1,0:T(8,128)} %refs_4_.5, bf16[768,512]{1,0:T(8,128)(2,1)S(1)} %broadcast_select_fusion.5.refs_3_, ...), custom_call_target="tpu_custom_call", output_to_operand_aliasing={{}: (5, {})} | custom-call | flops 9663676416 | bytes 9437184 | tf_op jit(solution)/shard_map/pallas_call | solution.py:124
  58.8 7.0 %collective-permute-done.4 = bf16[768,512]{1,0:T(8,128)(2,1)S(1)} collective-permute-done((bf16[768,512]{1,0:T(8,128)(2,1)S(1)}, bf16[768,512]{1,0:T(8,128)(2,1)S(1)}, u32[]{:S(2)}, u32[]{:S(2)}) %collective-permute-start.4) | collective-permute-done | bytes 786464 | tf_op jit(solution)/shard_map/ppermute | solution.py:228
  69.7 8.2 %shard_map.133.refs_5_ = f32[1536,512]{1,0:T(8,128)S(1)} custom-call(s32[23]{0:T(128)S(1)} %multiply_add_fusion.refs_0_, f32[1536,6144]{1,0:T(8,128)} %refs_4_.5, f32[1536,6144]{1,0:T(8,128)} %refs_4_.5, bf16[768,512]{1,0:T(8,128)(2,1)S(1)} %broadcast_select_fusion.6.refs_3_, ...), custom_call_target="tpu_custom_call", output_to_operand_aliasing={{}: (5, {})} | custom-call | flops 9663676416 | bytes 9437184 | tf_op jit(solution)/shard_map/pallas_call | solution.py:124
  77.9 5.6 %collective-permute-done.6.refs_7_ = bf16[768,512]{1,0:T(8,128)(2,1)S(1)} collective-permute-done((bf16[768,512]{1,0:T(8,128)(2,1)S(1)}, bf16[768,512]{1,0:T(8,128)(2,1)S(1)}, u32[]{:S(2)}, u32[]{:S(2)}) %collective-permute-start.6) | collective-permute-done | bytes 786464 | tf_op jit(solution)/shard_map/ppermute | solution.py:228
  85.2 5.9 %shard_map.134 = f32[1536,512]{1,0:T(8,128)S(1)} custom-call(s32[23]{0:T(128)S(1)} %multiply_add_fusion.refs_0_, f32[1536,6144]{1,0:T(8,128)} %refs_4_.5, f32[1536,6144]{1,0:T(8,128)} %refs_4_.5, bf16[384,512]{1,0:T(8,128)(2,1)S(1)} %get-tuple-element.100.refs_3_, bf16[384,512]{1,0:T(8,128)(2,1)S(1)} %get-tuple-element.97.refs_4_, ...), custom_call_target="tpu_custom_call", output_to_operand_aliasing={{}: (5, {})} | custom-call | flops 4831838208 | bytes 4718592 | tf_op jit(solution)/shard_map/pallas_call | solution.py:124
  97.9 13.6 %collective-permute-done.11.refs_11_.refs_12_ = bf16[768,512]{1,0:T(8,128)(2,1)S(1)} collective-permute-done((bf16[768,512]{1,0:T(8,128)(2,1)S(1)}, bf16[768,512]{1,0:T(8,128)(2,1)S(1)}, u32[]{:S(2)}, u32[]{:S(2)}) %collective-permute-start.11) | collective-permute-done | bytes 786464 | tf_op jit(solution)/shard_map/ppermute | solution.py:228
  111.6 3.5 %collective-permute-done.10.refs_9_.refs_10_ = bf16[768,512]{1,0:T(8,128)(2,1)S(1)} collective-permute-done((bf16[768,512]{1,0:T(8,128)(2,1)S(1)}, bf16[768,512]{1,0:T(8,128)(2,1)S(1)}, u32[]{:S(2)}, u32[]{:S(2)}) %collective-permute-start.10) | collective-permute-done | bytes 786464 | tf_op jit(solution)/shard_map/ppermute | solution.py:228
  117.5 13.6 %shard_map.136.refs_9_ = f32[1536,512]{1,0:T(8,128)S(1)} custom-call(s32[23]{0:T(128)S(1)} %multiply_add_fusion.refs_0_, f32[1536,6144]{1,0:T(8,128)} %refs_4_.5, f32[1536,6144]{1,0:T(8,128)} %refs_4_.5, f32[1536,6144]{1,0:T(8,128)} %refs_4_.5, f32[1536,6144]{1,0:T(8,128)} %refs_4_.5, f32[1536,6144]{1,0:T(8,128)} %refs_4_.5, ...), custom_call_target="tpu_custom_call", output_to_operand_aliasing={{}: (13, {})} | custom-call | flops 14495514624 | bytes 14155776 | tf_op jit(solution)/shard_map/pallas_call | solution.py:124
  131.1 4.5 %shard_map.135 = (f32[768,512]{1,0:T(8,128)}, f32[512,1024]{1,0:T(8,128)S(1)}) custom-call(f32[768,512]{1,0:T(8,128)S(1)} %add_select_fusion.grad, bf16[768,512]{1,0:T(8,128)(2,1)S(1)} %copy-done.8, bf16[768,512]{1,0:T(8,128)(2,1)S(1)} %copy-done.3, bf16[512,512]{1,0:T(8,128)(2,1)S(1)} %broadcast_select_fusion.8.top, f32[512,512]{1,0:T(8,128)S(1)} %copy-done.9, ...), custom_call_target="tpu_custom_call" | custom-call | flops 3221225472 | bytes 3145728 | tf_op jit(solution)/shard_map/pallas_call | solution.py:151
  138.9 9.7 %shard_map.137.refs_9_ = f32[1536,512]{1,0:T(8,128)S(1)} custom-call(s32[23]{0:T(128)S(1)} %multiply_add_fusion.refs_0_, f32[1536,6144]{1,0:T(8,128)} %refs_4_.5, f32[1536,6144]{1,0:T(8,128)} %refs_4_.5, f32[1536,6144]{1,0:T(8,128)} %refs_4_.5, f32[1536,6144]{1,0:T(8,128)} %refs_4_.5, ...), custom_call_target="tpu_custom_call", output_to_operand_aliasing={{}: (9, {})} | custom-call | flops 9663676416 | bytes 9437184 | tf_op jit(solution)/shard_map/pallas_call | solution.py:124
  148.6 4.5 %collective-permute-done.14.refs_5_.refs_6_ = bf16[768,512]{1,0:T(8,128)(2,1)S(1)} collective-permute-done((bf16[768,512]{1,0:T(8,128)(2,1)S(1)}, bf16[768,512]{1,0:T(8,128)(2,1)S(1)}, u32[]{:S(2)}, u32[]{:S(2)}) %collective-permute-start.14) | collective-permute-done | bytes 786464 | tf_op jit(solution)/shard_map/ppermute | solution.py:228
  154.4 9.7 %shard_map.138 = f32[1536,512]{1,0:T(8,128)S(1)} custom-call(s32[23]{0:T(128)S(1)} %multiply_add_fusion.refs_0_, f32[1536,6144]{1,0:T(8,128)} %refs_4_.5, f32[1536,6144]{1,0:T(8,128)} %refs_4_.5, f32[1536,6144]{1,0:T(8,128)} %refs_4_.5, f32[1536,6144]{1,0:T(8,128)} %refs_4_.5, ...), custom_call_target="tpu_custom_call", output_to_operand_aliasing={{}: (9, {})} | custom-call | flops 9663676416 | bytes 9437184 | tf_op jit(solution)/shard_map/pallas_call | solution.py:124
  165.6 2.3 convolution_negate_fusion.share
  171.0 2.6 %add_add_fusion.grad = f32[768,512]{1,0:T(8,128)S(1)} fusion(f32[768,512]{1,0:T(8,128)} %collective-permute-done.16, f32[1536,512]{1,0:T(8,128)S(1)} %shard_map.138, pred[]{:T(512)S(6)} %eq.79, f32[768,512]{1,0:T(8,128)S(1)} %copy-done.14, bf16[512,512]{1,0:T(8,128)(2,1)S(1)} %copy-done.6), kind=kOutput, calls=%fused_computation.2 | convolution fusion | flops 1209139200 | bytes 8388609 | tf_op jit(solution)/shard_map/dot_general | solution.py:12
  173.6 2.3 %shard_map.139 = (f32[768,512]{1,0:T(8,128)S(1)}, f32[512,512]{1,0:T(8,128)S(1)}) custom-call(f32[768,512]{1,0:T(8,128)S(1)} %add_add_fusion.grad, bf16[768,512]{1,0:T(8,128)(2,1)S(1)} %copy-done.4, f32[512,512]{1,0:T(8,128)S(1)} %convolution_negate_fusion.share, f32[512,512]{1,0:T(8,128)S(1)} %copy-done.11), custom_call_target="tpu_custom_call" | custom-call | flops 2013265920 | bytes 3145728 | tf_op jit(solution)/shard_map/pallas_call | solution.py:172
  177.3 7.8 %collective-permute-done.18 = f32[4,32,1024]{2,1,0:T(8,128)} collective-permute-done((f32[4,32,1024]{2,1,0:T(8,128)}, f32[4,32,1024]{2,1,0:T(8,128)}, u32[]{:S(2)}, u32[]{:S(2)}) %collective-permute-start.18) | collective-permute-done | bytes 524320 | tf_op jit(solution)/shard_map/ppermute | solution.py:64
  188.7 5.9 %collective-permute-done.19 = f32[2,32,1024]{2,1,0:T(8,128)S(1)} collective-permute-done((f32[2,32,1024]{2,1,0:T(8,128)S(1)}, f32[2,32,1024]{2,1,0:T(8,128)S(1)}, u32[]{:S(2)}, u32[]{:S(2)}) %collective-permute-start.19) | collective-permute-done | bytes 262176 | tf_op jit(solution)/shard_map/ppermute | solution.py:64
  197.0 5.6 %collective-permute-done.20 = f32[1,32,1024]{2,1,0:T(8,128)S(1)} collective-permute-done((f32[1,32,1024]{2,1,0:T(8,128)S(1)}, f32[1,32,1024]{2,1,0:T(8,128)S(1)}, u32[]{:S(2)}, u32[]{:S(2)}) %collective-permute-start.20) | collective-permute-done | bytes 131104 | tf_op jit(solution)/shard_map/ppermute | solution.py:64
  (162 shorter events, 68.1 us)
Async XLA Ops:
  3.5 24.0 %collective-permute-start = (bf16[768,512]{1,0:T(8,128)(2,1)}, bf16[768,512]{1,0:T(8,128)(2,1)}, u32[]{:S(2)}, u32[]{:S(2)}) collective-permute-start(bf16[768,512]{1,0:T(8,128)(2,1)} %get-tuple-element.90), channel_id=1, source_target_pairs={{0,4},{4,8},{8,12},{12,14},{14,10},{10,6},{6,2},{2,0},{1,5},{5,9},... | collective-permute-start | bytes 2359304 | tf_op jit(solution)/shard_map/ppermute | solution.py:228
  6.5 21.0 %collective-permute-start.1 = (bf16[768,512]{1,0:T(8,128)(2,1)}, bf16[768,512]{1,0:T(8,128)(2,1)}, u32[]{:S(2)}, u32[]{:S(2)}) collective-permute-start(bf16[768,512]{1,0:T(8,128)(2,1)} %get-tuple-element.90), channel_id=1, source_target_pairs={{4,0},{8,4},{12,8},{14,12},{10,14},{6,10},{2,6},{0,2},{5,1},{9,5},... | collective-permute-start | bytes 2359304 | tf_op jit(solution)/shard_map/ppermute | solution.py:228
  27.5 19.3 %collective-permute-start.2 = (bf16[768,512]{1,0:T(8,128)(2,1)}, bf16[768,512]{1,0:T(8,128)(2,1)S(1)}, u32[]{:S(2)}, u32[]{:S(2)}) collective-permute-start(bf16[768,512]{1,0:T(8,128)(2,1)} %collective-permute-done), channel_id=1, source_target_pairs={{0,4},{4,8},{8,12},{12,14},{14,10},{10,6},{6,2},{2,0},{1,5},{5,9},... | collective-permute-start | bytes 2359304 | tf_op jit(solution)/shard_map/ppermute | solution.py:228
  29.6 18.6 %collective-permute-start.3 = (bf16[768,512]{1,0:T(8,128)(2,1)}, bf16[768,512]{1,0:T(8,128)(2,1)S(1)}, u32[]{:S(2)}, u32[]{:S(2)}) collective-permute-start(bf16[768,512]{1,0:T(8,128)(2,1)} %collective-permute-done.1), channel_id=1, source_target_pairs={{4,0},{8,4},{12,8},{14,12},{10,14},{6,10},{2,6},{0,2},{5,1},{9,5},... | collective-permute-start | bytes 2359304 | tf_op jit(solution)/shard_map/ppermute | solution.py:228
  48.2 17.5 %collective-permute-start.4 = (bf16[768,512]{1,0:T(8,128)(2,1)S(1)}, bf16[768,512]{1,0:T(8,128)(2,1)S(1)}, u32[]{:S(2)}, u32[]{:S(2)}) collective-permute-start(bf16[768,512]{1,0:T(8,128)(2,1)S(1)} %collective-permute-done.2), channel_id=1, source_target_pairs={{0,4},{4,8},{8,12},{12,14},{14,10},{10,6},{6,2},{2,0},{1,5},{5,9},... | collective-permute-start | bytes 2359304 | tf_op jit(solution)/shard_map/ppermute | solution.py:228
  49.8 17.2 %collective-permute-start.5 = (bf16[768,512]{1,0:T(8,128)(2,1)S(1)}, bf16[768,512]{1,0:T(8,128)(2,1)S(1)}, u32[]{:S(2)}, u32[]{:S(2)}) collective-permute-start(bf16[768,512]{1,0:T(8,128)(2,1)S(1)} %collective-permute-done.3), channel_id=1, source_target_pairs={{4,0},{8,4},{12,8},{14,12},{10,14},{6,10},{2,6},{0,2},{5,1},{9,5},... | collective-permute-start | bytes 2359304 | tf_op jit(solution)/shard_map/ppermute | solution.py:228
  67.1 16.3 %collective-permute-start.6 = (bf16[768,512]{1,0:T(8,128)(2,1)S(1)}, bf16[768,512]{1,0:T(8,128)(2,1)S(1)}, u32[]{:S(2)}, u32[]{:S(2)}) collective-permute-start(bf16[768,512]{1,0:T(8,128)(2,1)S(1)} %pad_maximum_fusion.1), channel_id=1, source_target_pairs={{0,4},{4,8},{8,12},{12,14},{14,10},{10,6},{6,2},{2,0},{1,5},{5,9},... | collective-permute-start | bytes 2359304 | tf_op jit(solution)/shard_map/ppermute | solution.py:228
  68.9 16.1 %collective-permute-start.7 = (bf16[768,512]{1,0:T(8,128)(2,1)S(1)}, bf16[768,512]{1,0:T(8,128)(2,1)S(1)}, u32[]{:S(2)}, u32[]{:S(2)}) collective-permute-start(bf16[768,512]{1,0:T(8,128)(2,1)S(1)} %pad_maximum_fusion.2), channel_id=1, source_target_pairs={{4,0},{8,4},{12,8},{14,12},{10,14},{6,10},{2,6},{0,2},{5,1},{9,5},... | collective-permute-start | bytes 2359304 | tf_op jit(solution)/shard_map/ppermute | solution.py:228
  91.5 23.6 %collective-permute-start.8 = (f32[768,512]{1,0:T(8,128)S(1)}, f32[768,512]{1,0:T(8,128)S(1)}, u32[]{:S(2)}, u32[]{:S(2)}) collective-permute-start(f32[768,512]{1,0:T(8,128)S(1)} %slice_select_fusion.1), channel_id=1, source_target_pairs={{0,1},{1,0},{2,3},{3,2},{4,5},{5,4},{6,7},{7,6},{8,9},{9,8},{10,11... | collective-permute-start | bytes 4718600 | tf_op jit(solution)/shard_map/ppermute | solution.py:48
  91.6 20.0 %collective-permute-start.11 = (bf16[768,512]{1,0:T(8,128)(2,1)S(1)}, bf16[768,512]{1,0:T(8,128)(2,1)S(1)}, u32[]{:S(2)}, u32[]{:S(2)}) collective-permute-start(bf16[768,512]{1,0:T(8,128)(2,1)S(1)} %pad_maximum_fusion.4), channel_id=1, source_target_pairs={{4,0},{8,4},{12,8},{14,12},{10,14},{6,10},{2,6},{0,2},{5,1},{9,5},... | collective-permute-start | bytes 2359304 | tf_op jit(solution)/shard_map/ppermute | solution.py:228
  96.2 18.9 %collective-permute-start.10 = (bf16[768,512]{1,0:T(8,128)(2,1)S(1)}, bf16[768,512]{1,0:T(8,128)(2,1)S(1)}, u32[]{:S(2)}, u32[]{:S(2)}) collective-permute-start(bf16[768,512]{1,0:T(8,128)(2,1)S(1)} %pad_maximum_fusion.3), channel_id=1, source_target_pairs={{0,4},{4,8},{8,12},{12,14},{14,10},{10,6},{6,2},{2,0},{1,5},{5,9},... | collective-permute-start | bytes 2359304 | tf_op jit(solution)/shard_map/ppermute | solution.py:228
  115.4 20.3 %collective-permute-start.12 = (bf16[768,512]{1,0:T(8,128)(2,1)S(1)}, bf16[768,512]{1,0:T(8,128)(2,1)S(1)}, u32[]{:S(2)}, u32[]{:S(2)}) collective-permute-start(bf16[768,512]{1,0:T(8,128)(2,1)S(1)} %collective-permute-done.10.refs_9_.refs_10_), channel_id=1, source_target_pairs={{0,4},{4,8},{8,12},{12,14},{14,10},{10,6},{6,2},{2,0},{1,5},{5,9},... | collective-permute-start | bytes 2359304 | tf_op jit(solution)/shard_map/ppermute | solution.py:228
  117.1 18.6 %collective-permute-start.13 = (bf16[768,512]{1,0:T(8,128)(2,1)S(1)}, bf16[768,512]{1,0:T(8,128)(2,1)S(1)}, u32[]{:S(2)}, u32[]{:S(2)}) collective-permute-start(bf16[768,512]{1,0:T(8,128)(2,1)S(1)} %collective-permute-done.11.refs_11_.refs_12_), channel_id=1, source_target_pairs={{4,0},{8,4},{12,8},{14,12},{10,14},{6,10},{2,6},{0,2},{5,1},{9,5},... | collective-permute-start | bytes 2359304 | tf_op jit(solution)/shard_map/ppermute | solution.py:228
  135.7 17.4 %collective-permute-start.14 = (bf16[768,512]{1,0:T(8,128)(2,1)S(1)}, bf16[768,512]{1,0:T(8,128)(2,1)S(1)}, u32[]{:S(2)}, u32[]{:S(2)}) collective-permute-start(bf16[768,512]{1,0:T(8,128)(2,1)S(1)} %collective-permute-done.12.refs_5_.refs_6_), channel_id=1, source_target_pairs={{0,4},{4,8},{8,12},{12,14},{14,10},{10,6},{6,2},{2,0},{1,5},{5,9},... | collective-permute-start | bytes 2359304 | tf_op jit(solution)/shard_map/ppermute | solution.py:228
  137.3 17.0 %collective-permute-start.15 = (bf16[768,512]{1,0:T(8,128)(2,1)S(1)}, bf16[768,512]{1,0:T(8,128)(2,1)S(1)}, u32[]{:S(2)}, u32[]{:S(2)}) collective-permute-start(bf16[768,512]{1,0:T(8,128)(2,1)S(1)} %collective-permute-done.13.refs_7_.refs_8_), channel_id=1, source_target_pairs={{4,0},{8,4},{12,8},{14,12},{10,14},{6,10},{2,6},{0,2},{5,1},{9,5},... | collective-permute-start | bytes 2359304 | tf_op jit(solution)/shard_map/ppermute | solution.py:228
  138.9 28.9 %collective-permute-start.17 = (f32[8,32,1024]{2,1,0:T(8,128)}, f32[8,32,1024]{2,1,0:T(8,128)}, u32[]{:S(2)}, u32[]{:S(2)}) collective-permute-start(f32[8,32,1024]{2,1,0:T(8,128)} %select_bitcast_fusion), channel_id=1, source_target_pairs={{0,1},{1,0},{2,3},{3,2},{4,5},{5,4},{6,7},{7,6},{8,9},{9,8},{10,11... | collective-permute-start | bytes 3145736 | tf_op jit(solution)/shard_map/ppermute | solution.py:56
  170.4 14.7 %collective-permute-start.18 = (f32[4,32,1024]{2,1,0:T(8,128)}, f32[4,32,1024]{2,1,0:T(8,128)}, u32[]{:S(2)}, u32[]{:S(2)}) collective-permute-start(f32[4,32,1024]{2,1,0:T(8,128)} %select_bitcast_fusion.4), channel_id=1, source_target_pairs={{0,2},{2,0},{4,6},{6,4},{8,10},{10,8},{12,14},{14,12},{1,3},{3,1},... | collective-permute-start | bytes 1572872 | tf_op jit(solution)/shard_map/ppermute | solution.py:64
  176.8 11.3 %collective-permute-start.21 = (f32[8,32,512]{2,1,0:T(8,128)}, f32[8,32,512]{2,1,0:T(8,128)S(1)}, u32[]{:S(2)}, u32[]{:S(2)}) collective-permute-start(f32[8,32,512]{2,1,0:T(8,128)} %select_bitcast_fusion.3), channel_id=1, source_target_pairs={{0,1},{1,0},{2,3},{3,2},{4,5},{5,4},{6,7},{7,6},{8,9},{9,8},{10,11... | collective-permute-start | bytes 1572872 | tf_op jit(solution)/shard_map/ppermute | solution.py:56
  186.6 8.0 %collective-permute-start.19 = (f32[2,32,1024]{2,1,0:T(8,128)S(1)}, f32[2,32,1024]{2,1,0:T(8,128)S(1)}, u32[]{:S(2)}, u32[]{:S(2)}) collective-permute-start(f32[2,32,1024]{2,1,0:T(8,128)S(1)} %select_bitcast_fusion.6), channel_id=1, source_target_pairs={{0,4},{2,6},{4,0},{6,2},{8,12},{10,14},{12,8},{14,10},{1,5},{3,7},... | collective-permute-start | bytes 786440 | tf_op jit(solution)/shard_map/ppermute | solution.py:64
  188.3 8.0 %collective-permute-start.22 = (f32[4,32,512]{2,1,0:T(8,128)S(1)}, f32[4,32,512]{2,1,0:T(8,128)S(1)}, u32[]{:S(2)}, u32[]{:S(2)}) collective-permute-start(f32[4,32,512]{2,1,0:T(8,128)S(1)} %select_bitcast_fusion.5), channel_id=1, source_target_pairs={{0,2},{2,0},{4,6},{6,4},{8,10},{10,8},{12,14},{14,12},{1,3},{3,1},... | collective-permute-start | bytes 786440 | tf_op jit(solution)/shard_map/ppermute | solution.py:64
  194.7 8.0 %collective-permute-start.20 = (f32[1,32,1024]{2,1,0:T(8,128)S(1)}, f32[1,32,1024]{2,1,0:T(8,128)S(1)}, u32[]{:S(2)}, u32[]{:S(2)}) collective-permute-start(f32[1,32,1024]{2,1,0:T(8,128)S(1)} %select_bitcast_fusion.8), channel_id=1, source_target_pairs={{0,8},{2,10},{4,12},{6,14},{8,0},{10,2},{12,4},{14,6},{1,9},{3,11}... | collective-permute-start | bytes 393224 | tf_op jit(solution)/shard_map/ppermute | solution.py:64
  209.5 8.7 %collective-permute-start.29 = (f32[32,512]{1,0:T(8,128)S(1)}, f32[32,512]{1,0:T(8,128)S(1)}, u32[]{:S(2)}, u32[]{:S(2)}) collective-permute-start(f32[32,512]{1,0:T(8,128)S(1)} %slice.270), channel_id=1, source_target_pairs={{10,0},{11,1},{26,16},{27,17}} | collective-permute-start | bytes 196616 | tf_op jit(solution)/shard_map/ppermute | solution.py:291
  211.2 7.9 %collective-permute-start.30 = (f32[32,512]{1,0:T(8,128)S(1)}, f32[32,512]{1,0:T(8,128)S(1)}, u32[]{:S(2)}, u32[]{:S(2)}) collective-permute-start(f32[32,512]{1,0:T(8,128)S(1)} %slice.270), channel_id=1, source_target_pairs={{12,0},{13,1},{28,16},{29,17}} | collective-permute-start | bytes 196616 | tf_op jit(solution)/shard_map/ppermute | solution.py:291
  212.5 8.9 %collective-permute-start.31 = (f32[32,512]{1,0:T(8,128)S(1)}, f32[32,512]{1,0:T(8,128)S(1)}, u32[]{:S(2)}, u32[]{:S(2)}) collective-permute-start(f32[32,512]{1,0:T(8,128)S(1)} %slice.270), channel_id=1, source_target_pairs={{14,0},{15,1},{30,16},{31,17}} | collective-permute-start | bytes 196616 | tf_op jit(solution)/shard_map/ppermute | solution.py:291
  (28 other events, 215.3 us)

commit v2 on v1

--- a/solution.py
+++ b/solution.py
@@ -72,6 +72,28 @@
     return value[0]
 
 
+def join_cols(value, col_id):
+    other = lax.ppermute(value, "col", SWAP)
+    first = col_id == 0
+    return jnp.concatenate([jnp.where(first, value, other), jnp.where(first, other, value)], axis=0)
+
+
+def gather_blocks(value, row_id, col_id, n_rows):
+    half, width = value.shape
+    value = value[None]
+    bit = n_rows // 2
+    while bit:
+        other = lax.ppermute(value, "row", flip(n_rows, bit))
+        zero = (row_id & bit) == 0
+        value = jnp.stack([jnp.where(zero, value, other), jnp.where(zero, other, value)], axis=1)
+        value = value.reshape(-1, half, width)
+        bit //= 2
+    other = lax.ppermute(value, "col", SWAP)
+    first = col_id == 0
+    both = jnp.stack([jnp.where(first, value, other), jnp.where(first, other, value)], axis=1)
+    return both.reshape(-1, width)
+
+
 def split(value):
     coarse = value.astype(jnp.bfloat16)
     return coarse, (value - coarse.astype(jnp.float32)).astype(jnp.bfloat16)
@@ -95,34 +117,35 @@
     total, out = refs[2 * count], refs[-1]
     acc = total[...] if has_total else None
     for block, piece in zip(blocks, pieces):
-        for part in split(block[...]):
+        value = block[...]
+        coarse = value.astype(jnp.bfloat16)
+        fine = (value - coarse.astype(jnp.float32)).astype(jnp.bfloat16)
+        for part in (coarse, fine):
             term = jnp.dot(part, piece[...], preferred_element_type=jnp.float32)
             acc = term if acc is None else acc + term
     out[...] = acc
 
 
-def add_pieces(total, matrix, pieces, places):
-    rows, width = matrix.shape[0], pieces[0][0].shape[1]
+def add_pieces(total, matrix, pieces, places, first_place):
+    rows, width = matrix.shape[0], pieces[0].shape[1]
     tile = 512 if rows % 512 == 0 else 256
-
-    def columns(depth, index):
-        return pl.BlockSpec((tile, depth), lambda i, where: (i, where[index]))
-
-    def part(depth, block):
-        return pl.BlockSpec((depth, width), lambda i, where: (block, 0))
-
-    specs = [columns(depth, index) for _, _, depth, index in pieces]
-    specs += [part(depth, block) for _, block, depth, _ in pieces]
-    args = [matrix] * len(pieces) + [array for array, _, _, _ in pieces]
+    count = len(pieces)
+
+    def columns(which):
+        return pl.BlockSpec((tile, pieces[which].shape[0]), lambda i, where: (i, where[first_place + which]))
+
+    specs = [columns(k) for k in range(count)]
+    specs += [pl.BlockSpec(p.shape, lambda i, where: (0, 0)) for p in pieces]
+    args = [matrix] * count + list(pieces)
     line = pl.BlockSpec((tile, width), lambda i, where: (i, 0))
     aliases = {}
     if total is not None:
         aliases = {1 + len(args): 0}
         specs.append(line)
         args.append(total)
-    depth = sum(p[2] for p in pieces)
+    depth = sum(p.shape[0] for p in pieces)
     return pl.pallas_call(
-        lambda *refs: piece_kernel(len(pieces), total is not None, *refs),
+        lambda *refs: piece_kernel(count, total is not None, *refs),
         out_shape=jax.ShapeDtypeStruct((rows, width), jnp.float32),
         grid_spec=pltpu.PrefetchScalarGridSpec(
             num_scalar_prefetch=1, grid=(rows // tile,), in_specs=specs, out_specs=line
@@ -182,24 +205,40 @@
     )(grad, early, share, inv_early)
 
 
+class Ring:
+    def __init__(self, piece, n_rows):
+        order = ring_order(n_rows)
+        self.ahead = [(order[i], order[(i + 1) % n_rows]) for i in range(n_rows)]
+        self.back = [(b, a) for a, b in self.ahead]
+        self.n, self.half = n_rows, piece.shape[0] // 2
+        self.step = 0
+        self.held = (piece, piece)
+
+    def advance(self):
+        self.step += 1
+        before, after = self.held
+        if self.step == self.n // 2:
+            before, after = before[: self.half], after[self.half :]
+        before = lax.ppermute(before, "row", self.ahead)
+        after = lax.ppermute(after, "row", self.back)
+        self.held = lax.optimization_barrier((before, after))
+        return self.held
+
+
 def ring_places(n_rows, row_id):
     order = ring_order(n_rows)
     where = [0] * n_rows
     for place, row in enumerate(order):
         where[row] = place
-    entries = [(0, 1, 0)]
+    offsets = [0]
     for step in range(1, n_rows // 2):
-        entries += [(-step, 1, 0), (step, 1, 0)]
-    half_at = {}
-    for step in range(1, n_rows // 2 + 1):
-        for way, sign in ((0, -1), (1, 1)):
-            for half in (0, 1):
-                half_at[way, step, half] = len(entries)
-                entries.append((sign * step, 2, half))
-    offset, scale, shift = (jnp.array(part, jnp.int32) for part in zip(*entries))
+        offsets += [n_rows - step, step]
+    offsets += [n_rows // 2] * 2
     place = jnp.array(where, jnp.int32)[row_id]
-    owner = jnp.array(order, jnp.int32)[(place + offset + n_rows) % n_rows]
-    return owner, owner * scale + shift, half_at
+    whose = jnp.array(order, jnp.int32)[(place + jnp.array(offsets, jnp.int32)) % n_rows]
+    scale = jnp.array([1] * (n_rows - 1) + [2, 2], jnp.int32)
+    shift = jnp.array([0] * n_rows + [1], jnp.int32)
+    return whose, whose * scale + shift
 
 
 def by_ring(cot, late_masked, panel_early, inv_late, inv_early, trailing, own_start):
@@ -209,93 +248,74 @@
     piece_rows, width = late_masked.shape
     first = col_id == 0
     is_root = (row_id == 0) & first
-    owner, places, half_at = ring_places(n_rows, row_id)
+    whose, places = ring_places(n_rows, row_id)
     half = piece_rows // 2
-    mid = n_rows // 2
     local = jnp.arange(piece_rows, dtype=jnp.int32)[:, None]
-    order = ring_order(n_rows)
-    ahead = [(order[i], order[(i + 1) % n_rows]) for i in range(n_rows)]
-    ways = (ahead, [(b, a) for a, b in ahead])
-    tie = lax.optimization_barrier
-
-    def lead(value, way):
-        return value[:half] if way == 0 else value[half:]
-
-    def rest(value, way):
-        return value[half:] if way == 0 else value[:half]
-
-    def send(held):
-        return list(tie(tuple(lax.ppermute(h, "row", way) for h, way in zip(held, ways))))
-
-    def kept(piece, index, start):
-        zero = first & (owner[index] == 0) & (local[start : start + piece.shape[0]] < width)
-        return jnp.where(zero, jnp.zeros_like(piece), piece)
 
     sent = jnp.where(is_root & (local < width), panel_early, late_masked)
-    late_part = add_pieces(None, cot, [(late_masked, 0, piece_rows, 0)], places)
-    early_part = add_pieces(None, cot, [(panel_early, 0, piece_rows, 0)], places)
+
+    def kept(piece, owner, start):
+        lead = first & (owner == 0) & (local[start : start + piece.shape[0]] < width)
+        return jnp.where(lead, jnp.zeros_like(piece), piece)
+
+    ring = Ring(sent, n_rows)
+    late_part = add_pieces(None, cot, [late_masked], places, 0)
+    early_part = add_pieces(None, cot, [panel_early], places, 0)
     top = jnp.where(is_root, sent[:width], jnp.zeros_like(sent[:width]))
-    held = [sent, sent]
-    for step in range(1, mid):
-        held = send(held)
+    for step in range(1, n_rows // 2):
+        came = ring.advance()
         if step == 1:
-            late_part, *held = tie((late_part, *held))
-        else:
-            late_part, early_part, *held = tie((late_part, early_part, *held))
-        pieces = []
-        for way, piece in enumerate(held):
-            index = 2 * step - 1 + way
-            top = jnp.where(first & (owner[index] == 0), piece[:width], top)
-            pieces.append((kept(piece, index, 0), 0, piece_rows, index))
-        late_part = add_pieces(late_part, cot, pieces, places)
-
-    held = [jnp.concatenate([lead(h, w), lead(panel_early, w)]) for w, h in enumerate(held)]
-    held = send(held)
-    late_part, *held = tie((late_part, *held))
-    far = [half_at[0, mid, 0], half_at[1, mid, 1]]
-    whole = jnp.concatenate([h[:half] for h in held])
-    top = jnp.where(first & (owner[far[0]] == 0), whole[:width], top)
-    pieces = [(kept(h[:half], far[w], w * half), 0, half, far[w]) for w, h in enumerate(held)]
-    late_part = add_pieces(late_part, cot, pieces, places)
-    waiting = [(h, 1, half, half_at[w, 1, w]) for w, h in enumerate(held)]
-
-    for step in range(1, mid):
-        if step == 1:
-            held = [jnp.concatenate([rest(panel_early, w), h[half:]]) for w, h in enumerate(held)]
-        held = send(held)
-        if step == 1:
-            top = jnp.where(first, top, lax.ppermute(top, "col", [(0, 1)]))
-            late_grad = jnp.where(trailing, sum_cols(late_part, col_id), jnp.float32(0.0))
-            late_grad, top, *held = tie((late_grad, top, *held))
-            late_cot, both = late_chain(late_grad, late_masked, panel_early, top, inv_late, inv_early)
-            corner_cot = both[:, width:]
-        elif step == 2:
-            early_part, both, *held = tie((early_part, both, *held))
-            both = fold_cols(both, col_id, n_rows)
-        else:
-            early_part, *held = tie((early_part, *held))
-        for w, h in enumerate(held):
-            waiting.append((h, 0, half, half_at[w, step, 1 - w]))
-            waiting.append((h, 1, half, half_at[w, step + 1, w]))
-        early_part = add_pieces(early_part, cot, waiting, places)
-        waiting = []
-
-    both = scatter_rows(both, row_id, n_rows)
+            late_part, *came = lax.optimization_barrier((late_part, *came))
+        if step == 2:
+            early_part, *came = lax.optimization_barrier((early_part, *came))
+        ring.held = came
+        at = 2 * step - 1
+        for which, piece in enumerate(came):
+            top = jnp.where(first & (whose[at + which] == 0), piece[:width], top)
+        pieces = [kept(piece, whose[at + which], 0) for which, piece in enumerate(came)]
+        late_part = add_pieces(late_part, cot, pieces, places, at)
+    panel_next, *ring.held = lax.optimization_barrier((panel_early, *ring.held))
+    low, high_rows = ring.advance()
+    far = whose[n_rows - 1]
+    top = jnp.where(first & (far == 0), jnp.concatenate([low, high_rows], axis=0)[:width], top)
+    pieces = [kept(low, far, 0), kept(high_rows, far, half)]
+    late_part = add_pieces(late_part, cot, pieces, places, n_rows - 1)
+
+    ring = Ring(panel_next, n_rows)
+    top = jnp.where(first, top, lax.ppermute(top, "col", [(0, 1)]))
+    late_grad = jnp.where(trailing, sum_cols(late_part, col_id), jnp.float32(0.0))
+    late_cot, both = late_chain(late_grad, late_masked, panel_early, top, inv_late, inv_early)
+    corner_cot = both[:, width:]
     top_f = top.astype(jnp.float32)
     extra = high(late_cot, top_f)
     corner_share = -high(corner_cot, top_f, (0, 0))
+    both = fold_cols(both, col_id, n_rows)
+    bit = 1
+    for step in range(1, n_rows // 2 + 1):
+        came = ring.advance()
+        if step > 1:
+            early_part, *came = lax.optimization_barrier((early_part, *came))
+        if step > 2 and bit < n_rows:
+            both = scatter_step(both, row_id, n_rows, bit)
+            bit *= 2
+            both, *came = lax.optimization_barrier((both, *came))
+        ring.held = came
+        early_part = add_pieces(early_part, cot, came, places, 2 * step - 1)
+    while bit < n_rows:
+        both = scatter_step(both, row_id, n_rows, bit)
+        bit *= 2
+    both = both[0]
+    late_diag = join_cols(both[:, :width], col_id)
+    corner = gather_blocks(both[:, width:], row_id, col_id, n_rows)
+
     early_grad = sum_cols(early_part, col_id) + extra
     early_cot, early_term = early_chain(early_grad, panel_early, corner_share, inv_early)
-    early_own = scatter_rows(fold_cols(early_term, col_id, n_rows), row_id, n_rows)
-    own = both[:, width:]
-    blocks = [own] + [lax.ppermute(own, "row", [(k, 0)]) for k in range(1, n_rows)]
-    mine = jnp.stack([both[:, :width], early_own] + blocks)
-    other = lax.ppermute(mine, "col", SWAP)
-    joined = jnp.stack([jnp.where(first, mine, other), jnp.where(first, other, mine)], axis=1)
-    joined = joined.reshape(n_rows + 2, -1, width)
-    corner = jnp.where(is_root, joined[2:].reshape(width, width), jnp.float32(0.0))
-    early_cot = jnp.concatenate([early_cot[:width] + corner, early_cot[width:]], axis=0)
-    return (late_cot, early_cot, joined[0], joined[1])
+    early_diag = join_cols(
+        scatter_rows(fold_cols(early_term, col_id, n_rows), row_id, n_rows), col_id
+    )
+    top_rows = early_cot[:width] + jnp.where(is_root, corner, jnp.float32(0.0))
+    early_cot = jnp.concatenate([top_rows, early_cot[width:]], axis=0)
+    return (late_cot, early_cot, late_diag, early_diag)
 
 
 def by_gather(cot, late_masked, panel_early, inv_late, inv_early, trailing, own_start):

time: 227 us -> 222 us (0.978)
  waiting for transfers between devices: 75.3 us -> 82.5 us
  starting transfers between devices: 33.4 us -> 28.9 us
  other arithmetic: 20.4 us -> 16.8 us
  matrix products: 4.87 us -> 1.83 us
    ppermute x6, waiting for transfers between devices: 19.3 us -> 23.8 us  [scatter_step(): return kept + lax.ppermute(sent, 'row', flip(n_rows, bit))]
    ppermute x22, starting transfers between devices: 24.6 us -> 20.2 us  [the longest x8 11 us: advance(): before = lax.ppermute(before, 'row', self.ahead)]
    dot_general x2, matrix products: 4.87 us -> 1.83 us  [high(): lax.dot_general(left, right, (((contract[0],), (contract[1],)), ((), ()))...]
    ppermute x22, waiting for transfers between devices: 55.9 us -> 58.7 us  [the longest x8 29.8 us: advance(): before = lax.ppermute(before, 'row', self.ahead)]
    pallas_call x9 -> x10, Pallas kernels: 74 us -> 71.9 us  [add_pieces(): pl.pallas_call(lambda *refs: piece_kernel(count, total is not None, *refs...]
    select_n x9 -> x13, other arithmetic: 6.03 us -> 6.32 us  [the longest x8 3.58 us: kept(): return jnp.where(lead, jnp.zeros_like(piece), piece)]
  transfers between devices with their start and end apart: 33 -> 33, of which waited for: 20 -> 20; matrix products, arithmetic and copies ran while one was open for 9% -> 7% of each run, Pallas kernels for 33% -> 34%
where the time goes in v2:
time: 222 us; the launch traced here: 221 us
  waiting for transfers between devices  82.5 us (37%)
  Pallas kernels  81 us (36%)
  starting transfers between devices  28.9 us (13%)
  other arithmetic  16.8 us (8%)
  between operations  5.91 us (3%)
  local copies, waits for them, and re-layouts  4.2 us (2%)
    pallas_call x10, Pallas kernels, add_pieces(): pl.pallas_call(lambda *refs: piece_kernel(count, total is not None, *refs...  71.9 us
    ppermute x8, waiting for transfers between devices, advance(): before = lax.ppermute(before, 'row', self.ahead)  29.8 us
    ppermute x6, waiting for transfers between devices, scatter_step(): return kept + lax.ppermute(sent, 'row', flip(n_rows, bit))  23.8 us
    ppermute x8, waiting for transfers between devices, advance(): after = lax.ppermute(after, 'row', self.back)  15.5 us
    ppermute x8, starting transfers between devices, advance(): before = lax.ppermute(before, 'row', self.ahead)  11 us
    ppermute x3, waiting for transfers between devices, gather_blocks(): other = lax.ppermute(value, 'row', flip(n_rows, bit))  10.5 us
    ppermute x8, starting transfers between devices, advance(): after = lax.ppermute(after, 'row', self.back)  6.44 us
    ppermute x6, starting transfers between devices, scatter_step(): return kept + lax.ppermute(sent, 'row', flip(n_rows, bit))  6.01 us
  transfers between devices with their start and end apart: 33, of which 20 were waited for; matrix products, arithmetic and copies ran while one was open for 7% of the time, Pallas kernels for 34%

profile of v2, /device:TPU:0, one launch (start us, length us, event | category | flops | bytes accessed | tf_op | source)
XLA Modules:
  0.0 221.2 jit_solution(4292483368502755958)
XLA Ops:
  3.5 2.9 %collective-permute-start.1 = (bf16[768,512]{1,0:T(8,128)(2,1)}, bf16[768,512]{1,0:T(8,128)(2,1)}, u32[]{:S(2)}, u32[]{:S(2)}) collective-permute-start(bf16[768,512]{1,0:T(8,128)(2,1)} %get-tuple-element.92), channel_id=1, source_target_pairs={{4,0},{8,4},{12,8},{14,12},{10,14},{6,10},{2,6},{0,2},{5,1},{9,5},... | collective-permute-start | bytes 2359304 | tf_op jit(solution)/shard_map/ppermute | solution.py:223
  13.8 5.6 %shard_map.129.refs_5_ = f32[1536,512]{1,0:T(8,128)S(1)} custom-call(s32[9]{0:T(128)S(1)} %multiply_add_fusion.refs_0_, f32[1536,6144]{1,0:T(8,128)} %refs_2_.17, bf16[768,512]{1,0:T(8,128)(2,1)} %early.3), custom_call_target="tpu_custom_call" | custom-call | flops 4831838208 | bytes 4718592 | tf_op jit(solution)/shard_map/pallas_call | solution.py:147
  19.4 5.4 %shard_map.130.refs_5_ = f32[1536,512]{1,0:T(8,128)S(1)} custom-call(s32[9]{0:T(128)S(1)} %multiply_add_fusion.refs_0_, f32[1536,6144]{1,0:T(8,128)} %refs_2_.17, bf16[768,512]{1,0:T(8,128)(2,1)S(1)} %copy-done.4), custom_call_target="tpu_custom_call" | custom-call | flops 4831838208 | bytes 4718592 | tf_op jit(solution)/shard_map/pallas_call | solution.py:147
  30.5 8.2 %shard_map.131.refs_5_ = f32[1536,512]{1,0:T(8,128)S(1)} custom-call(s32[9]{0:T(128)S(1)} %multiply_add_fusion.refs_0_, f32[1536,6144]{1,0:T(8,128)} %refs_2_.17, f32[1536,6144]{1,0:T(8,128)} %refs_2_.17, bf16[768,512]{1,0:T(8,128)(2,1)S(1)} %broadcast_select_fusion.1.refs_3_, ...), custom_call_target="tpu_custom_call", output_to_operand_aliasing={{}: (5, {})} | custom-call | flops 9663676416 | bytes 9437184 | tf_op jit(solution)/shard_map/pallas_call | solution.py:147
  38.7 5.4 %collective-permute-done.2 = bf16[768,512]{1,0:T(8,128)(2,1)S(1)} collective-permute-done((bf16[768,512]{1,0:T(8,128)(2,1)}, bf16[768,512]{1,0:T(8,128)(2,1)S(1)}, u32[]{:S(2)}, u32[]{:S(2)}) %collective-permute-start.2) | collective-permute-done | bytes 786464 | tf_op jit(solution)/shard_map/ppermute | solution.py:222
  49.4 8.2 %shard_map.132.refs_5_ = f32[1536,512]{1,0:T(8,128)S(1)} custom-call(s32[9]{0:T(128)S(1)} %multiply_add_fusion.refs_0_, f32[1536,6144]{1,0:T(8,128)} %refs_2_.17, f32[1536,6144]{1,0:T(8,128)} %refs_2_.17, bf16[768,512]{1,0:T(8,128)(2,1)S(1)} %broadcast_select_fusion.3.refs_3_, ...), custom_call_target="tpu_custom_call", output_to_operand_aliasing={{}: (5, {})} | custom-call | flops 9663676416 | bytes 9437184 | tf_op jit(solution)/shard_map/pallas_call | solution.py:147
  57.5 6.9 %collective-permute-done.4 = bf16[768,512]{1,0:T(8,128)(2,1)S(1)} collective-permute-done((bf16[768,512]{1,0:T(8,128)(2,1)S(1)}, bf16[768,512]{1,0:T(8,128)(2,1)S(1)}, u32[]{:S(2)}, u32[]{:S(2)}) %collective-permute-start.4) | collective-permute-done | bytes 786464 | tf_op jit(solution)/shard_map/ppermute | solution.py:222
  68.8 8.2 %shard_map.133.refs_5_ = f32[1536,512]{1,0:T(8,128)S(1)} custom-call(s32[9]{0:T(128)S(1)} %multiply_add_fusion.refs_0_, f32[1536,6144]{1,0:T(8,128)} %refs_2_.17, f32[1536,6144]{1,0:T(8,128)} %refs_2_.17, bf16[768,512]{1,0:T(8,128)(2,1)S(1)} %broadcast_select_fusion.5.refs_3_, ...), custom_call_target="tpu_custom_call", output_to_operand_aliasing={{}: (5, {})} | custom-call | flops 9663676416 | bytes 9437184 | tf_op jit(solution)/shard_map/pallas_call | solution.py:147
  77.3 5.9 %shard_map.134 = f32[1536,512]{1,0:T(8,128)S(1)} custom-call(s32[9]{0:T(128)S(1)} %multiply_add_fusion.refs_0_, f32[1536,6144]{1,0:T(8,128)} %refs_2_.17, f32[1536,6144]{1,0:T(8,128)} %refs_2_.17, bf16[384,512]{1,0:T(8,128)(2,1)S(1)} %broadcast_select_fusion.10.refs_3_, ...), custom_call_target="tpu_custom_call", output_to_operand_aliasing={{}: (5, {})} | custom-call | flops 4831838208 | bytes 4718592 | tf_op jit(solution)/shard_map/pallas_call | solution.py:147
  91.9 5.6 %shard_map.135 = (f32[768,512]{1,0:T(8,128)}, f32[512,1024]{1,0:T(8,128)S(1)}) custom-call(f32[768,512]{1,0:T(8,128)S(1)} %add_select_fusion.grad, bf16[768,512]{1,0:T(8,128)(2,1)S(1)} %copy-done.4, bf16[768,512]{1,0:T(8,128)(2,1)} %early.3, bf16[512,512]{1,0:T(8,128)(2,1)S(1)} %broadcast_select_fusion.8.top, f32[512,512]{1,0:T(8,128)S(1)} %copy-done.5, ...), custom_call_target="tpu_custom_call" | custom-call | flops 3221225472 | bytes 3145728 | tf_op jit(solution)/shard_map/pallas_call | solution.py:174
  99.2 8.0 %collective-permute-done.13.refs_4_ = bf16[768,512]{1,0:T(8,128)(2,1)} collective-permute-done((bf16[768,512]{1,0:T(8,128)(2,1)}, bf16[768,512]{1,0:T(8,128)(2,1)}, u32[]{:S(2)}, u32[]{:S(2)}) %collective-permute-start.13) | collective-permute-done | bytes 786464 | tf_op jit(solution)/shard_map/ppermute | solution.py:223
  109.4 8.4 %shard_map.136.refs_5_ = f32[1536,512]{1,0:T(8,128)S(1)} custom-call(s32[9]{0:T(128)S(1)} %multiply_add_fusion.refs_0_, f32[1536,6144]{1,0:T(8,128)} %refs_2_.17, f32[1536,6144]{1,0:T(8,128)} %refs_2_.17, bf16[768,512]{1,0:T(8,128)(2,1)} %collective-permute-done.12.refs_3_, ...), custom_call_target="tpu_custom_call", output_to_operand_aliasing={{}: (5, {})} | custom-call | flops 9663676416 | bytes 9437184 | tf_op jit(solution)/shard_map/pallas_call | solution.py:147
  117.9 7.4 %collective-permute-done.14.refs_3_ = bf16[768,512]{1,0:T(8,128)(2,1)S(1)} collective-permute-done((bf16[768,512]{1,0:T(8,128)(2,1)}, bf16[768,512]{1,0:T(8,128)(2,1)S(1)}, u32[]{:S(2)}, u32[]{:S(2)}) %collective-permute-start.14) | collective-permute-done | bytes 786464 | tf_op jit(solution)/shard_map/ppermute | solution.py:222
  130.8 8.1 %shard_map.137.refs_5_ = f32[1536,512]{1,0:T(8,128)S(1)} custom-call(s32[9]{0:T(128)S(1)} %multiply_add_fusion.refs_0_, f32[1536,6144]{1,0:T(8,128)} %refs_2_.17, f32[1536,6144]{1,0:T(8,128)} %refs_2_.17, bf16[768,512]{1,0:T(8,128)(2,1)S(1)} %collective-permute-done.14.refs_3_, ...), custom_call_target="tpu_custom_call", output_to_operand_aliasing={{}: (5, {})} | custom-call | flops 9663676416 | bytes 9437184 | tf_op jit(solution)/shard_map/pallas_call | solution.py:147
  138.9 8.1 %collective-permute-done.16.refs_3_ = bf16[768,512]{1,0:T(8,128)(2,1)S(1)} collective-permute-done((bf16[768,512]{1,0:T(8,128)(2,1)S(1)}, bf16[768,512]{1,0:T(8,128)(2,1)S(1)}, u32[]{:S(2)}, u32[]{:S(2)}) %collective-permute-start.16) | collective-permute-done | bytes 786464 | tf_op jit(solution)/shard_map/ppermute | solution.py:222
  147.1 8.1 %collective-permute-done.11 = f32[4,32,1024]{2,1,0:T(8,128)S(1)} collective-permute-done((f32[4,32,1024]{2,1,0:T(8,128)S(1)}, f32[4,32,1024]{2,1,0:T(8,128)S(1)}, u32[]{:S(2)}, u32[]{:S(2)}) %collective-permute-start.11) | collective-permute-done | bytes 524320 | tf_op jit(solution)/shard_map/ppermute | solution.py:64
  157.6 8.2 %shard_map.138.refs_5_ = f32[1536,512]{1,0:T(8,128)S(1)} custom-call(s32[9]{0:T(128)S(1)} %multiply_add_fusion.refs_0_, f32[1536,6144]{1,0:T(8,128)} %refs_2_.17, f32[1536,6144]{1,0:T(8,128)} %refs_2_.17, bf16[768,512]{1,0:T(8,128)(2,1)S(1)} %collective-permute-done.16.refs_3_, ...), custom_call_target="tpu_custom_call", output_to_operand_aliasing={{}: (5, {})} | custom-call | flops 9663676416 | bytes 9437184 | tf_op jit(solution)/shard_map/pallas_call | solution.py:147
  170.1 5.9 %shard_map.139 = f32[1536,512]{1,0:T(8,128)S(1)} custom-call(s32[9]{0:T(128)S(1)} %multiply_add_fusion.refs_0_, f32[1536,6144]{1,0:T(8,128)} %refs_2_.17, f32[1536,6144]{1,0:T(8,128)} %refs_2_.17, bf16[384,512]{1,0:T(8,128)(2,1)S(1)} %collective-permute-done.19.refs_3_, ...), custom_call_target="tpu_custom_call", output_to_operand_aliasing={{}: (5, {})} | custom-call | flops 4831838208 | bytes 4718592 | tf_op jit(solution)/shard_map/pallas_call | solution.py:147
  180.9 5.7 %collective-permute-done.23 = f32[1,32,512]{2,1,0:T(8,128)S(1)} collective-permute-done((f32[1,32,512]{2,1,0:T(8,128)S(1)}, f32[1,32,512]{2,1,0:T(8,128)S(1)}, u32[]{:S(2)}, u32[]{:S(2)}) %collective-permute-start.23) | collective-permute-done | bytes 65568 | tf_op jit(solution)/shard_map/ppermute | solution.py:86
  187.8 3.9 %collective-permute-done.24 = f32[2,32,512]{2,1,0:T(8,128)S(1)} collective-permute-done((f32[2,32,512]{2,1,0:T(8,128)S(1)}, f32[2,32,512]{2,1,0:T(8,128)S(1)}, u32[]{:S(2)}, u32[]{:S(2)}) %collective-permute-start.24) | collective-permute-done | bytes 131104 | tf_op jit(solution)/shard_map/ppermute | solution.py:86
  193.6 3.4 %shard_map.140 = (f32[768,512]{1,0:T(8,128)S(1)}, f32[512,512]{1,0:T(8,128)S(1)}) custom-call(f32[768,512]{1,0:T(8,128)S(1)} %add_add_fusion.grad, bf16[768,512]{1,0:T(8,128)(2,1)} %early.3, f32[512,512]{1,0:T(8,128)S(1)} %convolution_negate_fusion.share, f32[512,512]{1,0:T(8,128)S(1)} %copy-done.7), custom_call_target="tpu_custom_call" | custom-call | flops 2013265920 | bytes 3145728 | tf_op jit(solution)/shard_map/pallas_call | solution.py:195
  201.0 7.1 %collective-permute-done.29 = f32[4,32,512]{2,1,0:T(8,128)S(1)} collective-permute-done((f32[4,32,512]{2,1,0:T(8,128)S(1)}, f32[4,32,512]{2,1,0:T(8,128)S(1)}, u32[]{:S(2)}, u32[]{:S(2)}) %collective-permute-start.29) | collective-permute-done | bytes 262176 | tf_op jit(solution)/shard_map/ppermute | solution.py:64
  208.8 4.5 %collective-permute-done.30 = f32[2,32,512]{2,1,0:T(8,128)S(1)} collective-permute-done((f32[2,32,512]{2,1,0:T(8,128)S(1)}, f32[2,32,512]{2,1,0:T(8,128)S(1)}, u32[]{:S(2)}, u32[]{:S(2)}) %collective-permute-start.30) | collective-permute-done | bytes 131104 | tf_op jit(solution)/shard_map/ppermute | solution.py:64
  215.0 4.1 %collective-permute-done.31 = f32[1,32,512]{2,1,0:T(8,128)S(1)} collective-permute-done((f32[1,32,512]{2,1,0:T(8,128)S(1)}, f32[1,32,512]{2,1,0:T(8,128)S(1)}, u32[]{:S(2)}, u32[]{:S(2)}) %collective-permute-start.31) | collective-permute-done | bytes 65568 | tf_op jit(solution)/shard_map/ppermute | solution.py:64
  (151 shorter events, 62.1 us)
Async XLA Ops:
  3.5 21.3 %collective-permute-start.1 = (bf16[768,512]{1,0:T(8,128)(2,1)}, bf16[768,512]{1,0:T(8,128)(2,1)}, u32[]{:S(2)}, u32[]{:S(2)}) collective-permute-start(bf16[768,512]{1,0:T(8,128)(2,1)} %get-tuple-element.92), channel_id=1, source_target_pairs={{4,0},{8,4},{12,8},{14,12},{10,14},{6,10},{2,6},{0,2},{5,1},{9,5},... | collective-permute-start | bytes 2359304 | tf_op jit(solution)/shard_map/ppermute | solution.py:223
  6.4 19.3 %collective-permute-start = (bf16[768,512]{1,0:T(8,128)(2,1)}, bf16[768,512]{1,0:T(8,128)(2,1)}, u32[]{:S(2)}, u32[]{:S(2)}) collective-permute-start(bf16[768,512]{1,0:T(8,128)(2,1)} %get-tuple-element.92), channel_id=1, source_target_pairs={{0,4},{4,8},{8,12},{12,14},{14,10},{10,6},{6,2},{2,0},{1,5},{5,9},... | collective-permute-start | bytes 2359304 | tf_op jit(solution)/shard_map/ppermute | solution.py:222
  25.8 18.3 %collective-permute-start.2 = (bf16[768,512]{1,0:T(8,128)(2,1)}, bf16[768,512]{1,0:T(8,128)(2,1)S(1)}, u32[]{:S(2)}, u32[]{:S(2)}) collective-permute-start(bf16[768,512]{1,0:T(8,128)(2,1)} %collective-permute-done), channel_id=1, source_target_pairs={{0,4},{4,8},{8,12},{12,14},{14,10},{10,6},{6,2},{2,0},{1,5},{5,9},... | collective-permute-start | bytes 2359304 | tf_op jit(solution)/shard_map/ppermute | solution.py:222
  28.2 18.7 %collective-permute-start.3 = (bf16[768,512]{1,0:T(8,128)(2,1)}, bf16[768,512]{1,0:T(8,128)(2,1)S(1)}, u32[]{:S(2)}, u32[]{:S(2)}) collective-permute-start(bf16[768,512]{1,0:T(8,128)(2,1)} %collective-permute-done.1), channel_id=1, source_target_pairs={{4,0},{8,4},{12,8},{14,12},{10,14},{6,10},{2,6},{0,2},{5,1},{9,5},... | collective-permute-start | bytes 2359304 | tf_op jit(solution)/shard_map/ppermute | solution.py:223
  46.9 17.5 %collective-permute-start.4 = (bf16[768,512]{1,0:T(8,128)(2,1)S(1)}, bf16[768,512]{1,0:T(8,128)(2,1)S(1)}, u32[]{:S(2)}, u32[]{:S(2)}) collective-permute-start(bf16[768,512]{1,0:T(8,128)(2,1)S(1)} %collective-permute-done.2), channel_id=1, source_target_pairs={{0,4},{4,8},{8,12},{12,14},{14,10},{10,6},{6,2},{2,0},{1,5},{5,9},... | collective-permute-start | bytes 2359304 | tf_op jit(solution)/shard_map/ppermute | solution.py:222
  48.7 17.6 %collective-permute-start.5 = (bf16[768,512]{1,0:T(8,128)(2,1)S(1)}, bf16[768,512]{1,0:T(8,128)(2,1)S(1)}, u32[]{:S(2)}, u32[]{:S(2)}) collective-permute-start(bf16[768,512]{1,0:T(8,128)(2,1)S(1)} %collective-permute-done.3), channel_id=1, source_target_pairs={{4,0},{8,4},{12,8},{14,12},{10,14},{6,10},{2,6},{0,2},{5,1},{9,5},... | collective-permute-start | bytes 2359304 | tf_op jit(solution)/shard_map/ppermute | solution.py:223
  66.4 10.6 %collective-permute-start.7 = (bf16[384,512]{1,0:T(8,128)(2,1)S(1)}, bf16[384,512]{1,0:T(8,128)(2,1)S(1)}, u32[]{:S(2)}, u32[]{:S(2)}) collective-permute-start(bf16[384,512]{1,0:T(8,128)(2,1)S(1)} %slice.163), channel_id=1, source_target_pairs={{4,0},{8,4},{12,8},{14,12},{10,14},{6,10},{2,6},{0,2},{5,1},{9,5},... | collective-permute-start | bytes 1179656 | tf_op jit(solution)/shard_map/ppermute | solution.py:223
  66.9 10.1 %collective-permute-start.6 = (bf16[384,512]{1,0:T(8,128)(2,1)S(1)}, bf16[384,512]{1,0:T(8,128)(2,1)S(1)}, u32[]{:S(2)}, u32[]{:S(2)}) collective-permute-start(bf16[384,512]{1,0:T(8,128)(2,1)S(1)} %slice.162), channel_id=1, source_target_pairs={{0,4},{4,8},{8,12},{12,14},{14,10},{10,6},{6,2},{2,0},{1,5},{5,9},... | collective-permute-start | bytes 1179656 | tf_op jit(solution)/shard_map/ppermute | solution.py:222
  83.5 6.6 %collective-permute-start.8 = (f32[768,512]{1,0:T(8,128)S(1)}, f32[768,512]{1,0:T(8,128)S(1)}, u32[]{:S(2)}, u32[]{:S(2)}) collective-permute-start(f32[768,512]{1,0:T(8,128)S(1)} %slice_select_fusion.1), channel_id=1, source_target_pairs={{0,1},{1,0},{2,3},{3,2},{4,5},{5,4},{6,7},{7,6},{8,9},{9,8},{10,11... | collective-permute-start | bytes 4718600 | tf_op jit(solution)/shard_map/ppermute | solution.py:48
  88.0 19.2 %collective-permute-start.13 = (bf16[768,512]{1,0:T(8,128)(2,1)}, bf16[768,512]{1,0:T(8,128)(2,1)}, u32[]{:S(2)}, u32[]{:S(2)}) collective-permute-start(bf16[768,512]{1,0:T(8,128)(2,1)} %early.3), channel_id=1, source_target_pairs={{4,0},{8,4},{12,8},{14,12},{10,14},{6,10},{2,6},{0,2},{5,1},{9,5},... | collective-permute-start | bytes 2359304 | tf_op jit(solution)/shard_map/ppermute | solution.py:223
  88.5 18.9 %collective-permute-start.12 = (bf16[768,512]{1,0:T(8,128)(2,1)}, bf16[768,512]{1,0:T(8,128)(2,1)}, u32[]{:S(2)}, u32[]{:S(2)}) collective-permute-start(bf16[768,512]{1,0:T(8,128)(2,1)} %early.3), channel_id=1, source_target_pairs={{0,4},{4,8},{8,12},{12,14},{14,10},{10,6},{6,2},{2,0},{1,5},{5,9},... | collective-permute-start | bytes 2359304 | tf_op jit(solution)/shard_map/ppermute | solution.py:222
  99.2 29.4 %collective-permute-start.10 = (f32[8,32,1024]{2,1,0:T(8,128)}, f32[8,32,1024]{2,1,0:T(8,128)}, u32[]{:S(2)}, u32[]{:S(2)}) collective-permute-start(f32[8,32,1024]{2,1,0:T(8,128)} %select_bitcast_fusion), channel_id=1, source_target_pairs={{0,1},{1,0},{2,3},{3,2},{4,5},{5,4},{6,7},{7,6},{8,9},{9,8},{10,11... | collective-permute-start | bytes 3145736 | tf_op jit(solution)/shard_map/ppermute | solution.py:56
  107.4 17.9 %collective-permute-start.14 = (bf16[768,512]{1,0:T(8,128)(2,1)}, bf16[768,512]{1,0:T(8,128)(2,1)S(1)}, u32[]{:S(2)}, u32[]{:S(2)}) collective-permute-start(bf16[768,512]{1,0:T(8,128)(2,1)} %collective-permute-done.12.refs_3_), channel_id=1, source_target_pairs={{0,4},{4,8},{8,12},{12,14},{14,10},{10,6},{6,2},{2,0},{1,5},{5,9},... | collective-permute-start | bytes 2359304 | tf_op jit(solution)/shard_map/ppermute | solution.py:222
  109.0 17.6 %collective-permute-start.15 = (bf16[768,512]{1,0:T(8,128)(2,1)}, bf16[768,512]{1,0:T(8,128)(2,1)S(1)}, u32[]{:S(2)}, u32[]{:S(2)}) collective-permute-start(bf16[768,512]{1,0:T(8,128)(2,1)} %collective-permute-done.13.refs_4_), channel_id=1, source_target_pairs={{4,0},{8,4},{12,8},{14,12},{10,14},{6,10},{2,6},{0,2},{5,1},{9,5},... | collective-permute-start | bytes 2359304 | tf_op jit(solution)/shard_map/ppermute | solution.py:223
  126.6 20.5 %collective-permute-start.16 = (bf16[768,512]{1,0:T(8,128)(2,1)S(1)}, bf16[768,512]{1,0:T(8,128)(2,1)S(1)}, u32[]{:S(2)}, u32[]{:S(2)}) collective-permute-start(bf16[768,512]{1,0:T(8,128)(2,1)S(1)} %collective-permute-done.14.refs_3_), channel_id=1, source_target_pairs={{0,4},{4,8},{8,12},{12,14},{14,10},{10,6},{6,2},{2,0},{1,5},{5,9},... | collective-permute-start | bytes 2359304 | tf_op jit(solution)/shard_map/ppermute | solution.py:222
  128.0 19.1 %collective-permute-start.17 = (bf16[768,512]{1,0:T(8,128)(2,1)S(1)}, bf16[768,512]{1,0:T(8,128)(2,1)S(1)}, u32[]{:S(2)}, u32[]{:S(2)}) collective-permute-start(bf16[768,512]{1,0:T(8,128)(2,1)S(1)} %collective-permute-done.15.refs_4_), channel_id=1, source_target_pairs={{4,0},{8,4},{12,8},{14,12},{10,14},{6,10},{2,6},{0,2},{5,1},{9,5},... | collective-permute-start | bytes 2359304 | tf_op jit(solution)/shard_map/ppermute | solution.py:223
  130.2 25.0 %collective-permute-start.11 = (f32[4,32,1024]{2,1,0:T(8,128)S(1)}, f32[4,32,1024]{2,1,0:T(8,128)S(1)}, u32[]{:S(2)}, u32[]{:S(2)}) collective-permute-start(f32[4,32,1024]{2,1,0:T(8,128)S(1)} %select_bitcast_fusion.4), channel_id=1, source_target_pairs={{0,2},{2,0},{4,6},{6,4},{8,10},{10,8},{12,14},{14,12},{1,3},{3,1},... | collective-permute-start | bytes 1572872 | tf_op jit(solution)/shard_map/ppermute | solution.py:64
  155.4 10.3 %collective-permute-start.18 = (f32[2,32,1024]{2,1,0:T(8,128)S(1)}, f32[2,32,1024]{2,1,0:T(8,128)S(1)}, u32[]{:S(2)}, u32[]{:S(2)}) collective-permute-start(f32[2,32,1024]{2,1,0:T(8,128)S(1)} %select_bitcast_fusion.8), channel_id=1, source_target_pairs={{0,4},{2,6},{4,0},{6,2},{8,12},{10,14},{12,8},{14,10},{1,5},{3,7},... | collective-permute-start | bytes 786440 | tf_op jit(solution)/shard_map/ppermute | solution.py:64
  155.5 11.1 %collective-permute-start.19 = (bf16[384,512]{1,0:T(8,128)(2,1)S(1)}, bf16[384,512]{1,0:T(8,128)(2,1)S(1)}, u32[]{:S(2)}, u32[]{:S(2)}) collective-permute-start(bf16[384,512]{1,0:T(8,128)(2,1)S(1)} %slice.187), channel_id=1, source_target_pairs={{0,4},{4,8},{8,12},{12,14},{14,10},{10,6},{6,2},{2,0},{1,5},{5,9},... | collective-permute-start | bytes 1179656 | tf_op jit(solution)/shard_map/ppermute | solution.py:222
  157.5 10.5 %collective-permute-start.20 = (bf16[384,512]{1,0:T(8,128)(2,1)S(1)}, bf16[384,512]{1,0:T(8,128)(2,1)S(1)}, u32[]{:S(2)}, u32[]{:S(2)}) collective-permute-start(bf16[384,512]{1,0:T(8,128)(2,1)S(1)} %slice.188), channel_id=1, source_target_pairs={{4,0},{8,4},{12,8},{14,12},{10,14},{6,10},{2,6},{0,2},{5,1},{9,5},... | collective-permute-start | bytes 1179656 | tf_op jit(solution)/shard_map/ppermute | solution.py:223
  168.0 8.4 %collective-permute-start.22 = (f32[1,32,1024]{2,1,0:T(8,128)S(1)}, f32[1,32,1024]{2,1,0:T(8,128)S(1)}, u32[]{:S(2)}, u32[]{:S(2)}) collective-permute-start(f32[1,32,1024]{2,1,0:T(8,128)S(1)} %select_bitcast_fusion.12), channel_id=1, source_target_pairs={{0,8},{2,10},{4,12},{6,14},{8,0},{10,2},{12,4},{14,6},{1,9},{3,11}... | collective-permute-start | bytes 393224 | tf_op jit(solution)/shard_map/ppermute | solution.py:64
  176.4 16.0 %collective-permute-start.21 = (f32[768,512]{1,0:T(8,128)S(1)}, f32[768,512]{1,0:T(8,128)S(1)}, u32[]{:S(2)}, u32[]{:S(2)}) collective-permute-start(f32[768,512]{1,0:T(8,128)S(1)} %slice_select_fusion), channel_id=1, source_target_pairs={{0,1},{1,0},{2,3},{3,2},{4,5},{5,4},{6,7},{7,6},{8,9},{9,8},{10,11... | collective-permute-start | bytes 4718600 | tf_op jit(solution)/shard_map/ppermute | solution.py:48
  180.0 6.6 %collective-permute-start.23 = (f32[1,32,512]{2,1,0:T(8,128)S(1)}, f32[1,32,512]{2,1,0:T(8,128)S(1)}, u32[]{:S(2)}, u32[]{:S(2)}) collective-permute-start(f32[1,32,512]{2,1,0:T(8,128)S(1)} %get-tuple-element.106), channel_id=1, source_target_pairs={{0,8},{2,10},{4,12},{6,14},{8,0},{10,2},{12,4},{14,6},{1,9},{3,11}... | collective-permute-start | bytes 196616 | tf_op jit(solution)/shard_map/ppermute | solution.py:86
  199.3 8.7 %collective-permute-start.29 = (f32[4,32,512]{2,1,0:T(8,128)S(1)}, f32[4,32,512]{2,1,0:T(8,128)S(1)}, u32[]{:S(2)}, u32[]{:S(2)}) collective-permute-start(f32[4,32,512]{2,1,0:T(8,128)S(1)} %select_bitcast_fusion.5), channel_id=1, source_target_pairs={{0,2},{2,0},{4,6},{6,4},{8,10},{10,8},{12,14},{14,12},{1,3},{3,1},... | collective-permute-start | bytes 786440 | tf_op jit(solution)/shard_map/ppermute | solution.py:64
  (23 other events, 140.1 us)
